TPU v7x, 128 devices: a whole 4x4x4 slice. The times are simulated.
128 devices in a mesh: seq: 8 (over z, core), dp: 16 (over y, x).
Axes of the slice: x: 4, y: 4, z: 4, core: 2. Of those that a mesh axis runs over, the one named last changes fastest.
Arguments:
- activations: bfloat16 [32768, 32768], P(('seq', 'dp')), may hold values from -180 to 180
- start_panel: bfloat16 [32768, 128], P(('seq', 'dp')), may hold values from -6 to 6
Outputs:
- new_panel: bfloat16 [32768, 128], P(('seq', 'dp'))
- sketch: float32 [32768, 128], P(('seq', 'dp'))
All inputs are finite; a program needn't handle non-finite values.
Results may differ from a plain program's by a relative error of at most 0.0071.
Values may be sent and summed in bfloat16 or wider, within the bound.
A program may use at most 128 MiB of HBM per device.

v0:
```python
import math

import jax
import jax.numpy as jnp
from jax import lax
from jax.sharding import PartitionSpec as P

NS_STEPS = 12


def shrink(ritz_gram, rank_cols):
    shift_mean = jnp.trace(ritz_gram) / rank_cols
    shifted = ritz_gram - shift_mean * jnp.eye(rank_cols, dtype=jnp.float32)
    scale_norm = jnp.sqrt(jnp.sum(shifted * shifted)) + 1e-06
    sign_iter = shifted / scale_norm
    for sweep in range(NS_STEPS):
        square = jnp.dot(sign_iter, sign_iter, precision=lax.Precision.HIGHEST)
        cube = jnp.dot(square, sign_iter, precision=lax.Precision.HIGHEST)
        sign_iter = 0.5 * (3.0 * sign_iter - cube)
    positive = 0.5 * (shifted + jnp.dot(shifted, sign_iter, precision=lax.Precision.HIGHEST))
    return (positive, shift_mean)


def orthonormal(pulled, cross_gram):
    factor_low = jnp.linalg.cholesky(cross_gram)
    return lax.linalg.triangular_solve(
        factor_low, pulled, left_side=False, lower=True, transpose_a=True
    )


def local(activations, start_panel):
    row_count, feature_count = activations.shape
    rank_cols = start_panel.shape[1]

    def add_block(piece):
        return jnp.dot(activations, piece, preferred_element_type=jnp.float32)

    projected = add_block(lax.all_gather(start_panel, ("seq", "dp"), axis=0, tiled=True)).astype(
        jnp.bfloat16
    )
    pulled = lax.psum_scatter(
        lax.dot_general(
            activations, projected, (((0,), (0,)), ((), ())), preferred_element_type=jnp.float32
        ),
        ("seq", "dp"),
        scatter_dimension=0,
        tiled=True,
    )
    local_gram = jnp.dot(pulled.T, pulled, precision=lax.Precision.HIGHEST)
    cross_gram = lax.psum(local_gram, ("seq", "dp"))
    new_panel = orthonormal(pulled, cross_gram).astype(jnp.bfloat16)
    mapped = add_block(lax.all_gather(new_panel, ("seq", "dp"), axis=0, tiled=True))
    local_ritz = jnp.dot(mapped.T, mapped, precision=lax.Precision.HIGHEST)
    ritz_gram = lax.psum(local_ritz, ("seq", "dp"))
    positive, shift_mean = shrink(ritz_gram, rank_cols)
    sketch = (
        math.sqrt(feature_count)
        / shift_mean
        * jnp.dot(new_panel.astype(jnp.float32), positive, precision=lax.Precision.HIGHEST)
    )
    return (new_panel, sketch)


def solution(mesh):
    in_specs = (P(("seq", "dp"), None), P(("seq", "dp"), None))
    out_specs = (P(("seq", "dp"), None), P(("seq", "dp"), None))
    return jax.shard_map(local, mesh=mesh, in_specs=in_specs, out_specs=out_specs, check_vma=False)
```

profile of v0, /device:TPU:1, one launch (start us, length us, event | category | flops | bytes accessed | tf_op | source)
XLA Modules:
  0.0 1179.8 jit_solution(5533589015763675452)
XLA Ops:
  7.2 0.7 all-gather.3.cloned.1.call-update
  7.9 77.0 %all-gather.3.cloned.1.call-done = bf16[32768,128]{1,0:T(8,128)(2,1)} async-done(((bf16[256,128]{1,0:T(8,128)(2,1)}), bf16[32768,128]{1,0:T(8,128)(2,1)}) %all-gather.3.cloned.1.call-update) | async-done | bytes 8388624 | tf_op jit(solution)/shard_map/all_gather | solution.py:38
  85.0 12.8 %convolution_convert_fusion = bf16[256,128]{1,0:T(8,128)(2,1)S(1)} fusion(bf16[256,32768]{1,0:T(8,128)(2,1)} %param.2, bf16[32768,128]{1,0:T(8,128)(2,1)} %all-gather.3.cloned.1.call-done), kind=kOutput, calls=%fused_computation.3 | convolution fusion | flops 2147516416 | bytes 25231360 | tf_op jit(solution)/shard_map/dot_general | solution.py:36
  97.9 8.1 convolution_bitcast_fusion
  106.1 640.9 %reduce-scatter.2.cloned.1.call-done = f32[256,128]{0,1:T(8,128)} async-done(((f32[32768,128]{0,1:T(8,128)}), f32[256,128]{0,1:T(8,128)}) %reduce-scatter.2.cloned.1.call-update) | async-done | bytes 131088 | tf_op jit(solution)/shard_map/reduce_scatter | solution.py:41
  746.9 1.9 fusion.91
  749.1 167.2 %all-reduce.3.cloned.1.call-done = f32[128,128]{0,1:T(8,128)} async-done(((f32[128,128]{0,1:T(8,128)}), f32[128,128]{0,1:T(8,128)}) %all-reduce.3.cloned.1.call-update) | async-done | bytes 65552 | tf_op jit(solution)/shard_map/psum | solution.py:50
  916.3 0.9 copy.5
  917.2 0.9 fusion.4
  918.1 11.7 cholesky.18
  929.8 0.6 compare_reduce_fusion
  930.4 0.7 fusion.2
  931.1 9.8 custom-call.6
  940.9 1.9 convolution_convert_fusion.1
  943.2 67.3 %all-gather.5.cloned.1.call-done = bf16[32768,128]{1,0:T(8,128)(2,1)} async-done(((bf16[256,128]{1,0:T(8,128)(2,1)}), bf16[32768,128]{1,0:T(8,128)(2,1)}) %all-gather.5.cloned.1.call-update) | async-done | bytes 8388624 | tf_op jit(solution)/shard_map/all_gather | solution.py:52
  1010.5 13.7 %fusion.92 = f32[128,256]{1,0:T(8,128)S(1)} fusion(bf16[32768,128]{1,0:T(8,128)(2,1)} %all-gather.5.cloned.1.call-done, bf16[256,32768]{1,0:T(8,128)(2,1)} %param.2), kind=kOutput, calls=%fused_computation.116 | convolution fusion | flops 2147483648 | bytes 25296896 | tf_op jit(solution)/shard_map/dot_general | solution.py:36
  1024.2 0.9 fusion.93
  1025.1 135.0 %all-reduce.5.cloned.1.call-done = f32[128,128]{1,0:T(8,128)} async-done(((f32[128,128]{1,0:T(8,128)}), f32[128,128]{1,0:T(8,128)}) %all-reduce.5.cloned.1.call-update) | async-done | bytes 65552 | tf_op jit(solution)/shard_map/psum | solution.py:54
  1160.1 1.5 select_reduce_fusion
  1162.2 1.5 multiply_reduce_fusion
  1164.4 1.1 fusion.63
  1165.5 1.1 convolution_subtract_fusion.11
  1171.3 1.0 fusion
  1172.4 0.9 convolution_multiply_fusion
  (36 shorter events, 5.3 us)
Async XLA Ops:
  7.2 77.8 %all-gather.3.cloned.1.call-start = ((), (), s32[]{:S(2)}) async-start(), calls=%async_computation.1 | async-start | bytes 8454144 | tf_op jit(solution)/shard_map/all_gather | solution.py:38
  7.9 739.0 %reduce-scatter.2.cloned.1.call-start = ((), (), s32[]{:S(2)}) async-start(), calls=%async_computation.2 | async-start | bytes 16908288 | tf_op jit(solution)/shard_map/reduce_scatter | solution.py:41
  85.0 12.9 %copy-start = (bf16[256,32768]{1,0:T(8,128)(2,1)S(1)}, bf16[256,32768]{1,0:T(8,128)(2,1)}, u32[]{:S(2)}) copy-start(bf16[256,32768]{1,0:T(8,128)(2,1)} %param.2) | copy-start | bytes 50331652
  106.0 810.2 %all-reduce.3.cloned.1.call-start = ((), (), s32[]{:S(2)}) async-start(), calls=%async_computation.3 | async-start | bytes 131072 | tf_op jit(solution)/shard_map/psum | solution.py:50
  748.8 261.6 %all-gather.5.cloned.1.call-start = ((), (), s32[]{:S(2)}) async-start(), calls=%async_computation.4 | async-start | bytes 8454144 | tf_op jit(solution)/shard_map/all_gather | solution.py:52
  942.9 229.5 %copy-start.1 = (bf16[256,128]{1,0:T(8,128)(2,1)S(1)}, bf16[256,128]{1,0:T(8,128)(2,1)}, u32[]{:S(2)}) copy-start(bf16[256,128]{1,0:T(8,128)(2,1)} %convolution_convert_fusion.1) | copy-start | bytes 196612
  942.9 217.2 %all-reduce.5.cloned.1.call-start = ((), (), s32[]{:S(2)}) async-start(), calls=%async_computation.5 | async-start | bytes 131072 | tf_op jit(solution)/shard_map/psum | solution.py:54
Sparse Core Ops, SparseCore 0:
  11.1 73.7 all-gather.2
  106.1 640.7 reduce-scatter.1
  752.2 163.9 all-reduce.2
  943.0 67.4 all-gather.4
  1025.2 134.8 all-reduce.4
where the time goes:
time: 1180 us
  waiting for transfers between devices  1090 us (92%)
  matrix products  48 us (4%)
  other arithmetic  26.6 us (2%)
  between operations  15.4 us (1%)
    reduce_scatter x1, waiting for transfers between devices, local(): lax.psum_scatter(lax.dot_general(activations, projected, (((0,), (0,)), (...  641 us
    psum x1, waiting for transfers between devices, local(): cross_gram = lax.psum(local_gram, ('seq', 'dp'))  167 us
    psum x1, waiting for transfers between devices, local(): ritz_gram = lax.psum(local_ritz, ('seq', 'dp'))  135 us
    all_gather x1, waiting for transfers between devices, local(): lax.all_gather(start_panel, ('seq', 'dp'), axis=0, tiled=True)  77 us
    all_gather x1, waiting for transfers between devices, local(): lax.all_gather(new_panel, ('seq', 'dp'), axis=0, tiled=True)  67.3 us
    dot_general x2, matrix products, add_block(): return jnp.dot(activations, piece, preferred_element_type=jnp.float32)  26.5 us
  transfers between devices with their start and end apart: 5, of which 5 were waited for; matrix products, arithmetic and copies ran while one was open for 0% of the time, Pallas kernels for 0%

commit v1 on v0

v1 whole, which is shorter than its diff:
```python
import functools
import math

import jax
import jax.numpy as jnp
from jax import lax
from jax.experimental import pallas as pl
from jax.experimental.pallas import tpu as pltpu
from jax.sharding import PartitionSpec as P

NS_STEPS = 12
MESH = pl.DeviceIdType.MESH
F32, BF16 = jnp.float32, jnp.bfloat16
HIGHEST = lax.Precision.HIGHEST
ORDERS = (("x", "y", "z"), ("z", "x", "y"), ("y", "z", "x"))
START_PARTS = ((0, 96), (96, 80), (176, 80))
PANEL_PARTS = ((0, 48), (48, 48), (96, 32))
N_SEMS = 256


def dot(a, b, dims=(((1,), (0,)), ((), ())), precision=None):
    return lax.dot_general(a, b, dims, precision=precision, preferred_element_type=F32)


class Links:
    def __init__(self, send_sems, recv_sems):
        seq, dp = lax.axis_index("seq"), lax.axis_index("dp")
        self.pos = dict(z=seq // 2, c=seq % 2, y=dp // 4, x=dp % 4)
        self.seq, self.dp = seq, dp
        self.send_sems, self.recv_sems, self.used, self.sent = send_sems, recv_sems, 0, []

    def at(self, axis, step):
        return lax.rem(self.pos[axis] + step, 4)

    def device(self, **other):
        p = {**self.pos, **other}
        return (p["z"] * 2 + p["c"], p["y"] * 4 + p["x"])

    def copy(self, src, dst, device):
        i = self.used
        self.used += 1
        made = pltpu.make_async_remote_copy(
            src_ref=src,
            dst_ref=dst,
            send_sem=self.send_sems.at[i],
            recv_sem=self.recv_sems.at[i],
            device_id=device,
            device_id_type=MESH,
        )
        made.start()
        self.sent.append(made)
        return made

    def drain(self):
        for made in self.sent:
            made.wait_send()
        self.sent = []


def gather(links, buf, parts, orders):
    pos, every = links.pos, slice(None)

    def region(part, **index):
        p = {**pos, **index}
        return buf.at[p["c"], p["z"], p["y"], p["x"], pl.ds(*part), :]

    def send(part, axis, step, **index):
        src = region(part, **index)
        return links.copy(src, src, links.device(**{axis: links.at(axis, step)}))

    first, second, third = [], [], [{k: [] for k in (1, 2, 3)} for _ in orders]
    planes = []
    for part, (a, b, c) in zip(parts, orders):
        first.append([send(part, a, k) for k in (1, 3, 2)])
    for o, (part, (a, b, c)) in enumerate(zip(parts, orders)):
        for made in first[o]:
            made.wait_recv()
        row = {a: every}
        second.append([send(part, b, k, **row) for k in (1, 3, 2)])
        for k in (1, 3, 2):
            third[o][k].append(send(part, c, k, **row))
    for j, step in enumerate((1, 3, 2)):
        for o, (part, (a, b, c)) in enumerate(zip(parts, orders)):
            second[o][j].wait_recv()
            row = {a: every, b: links.at(b, 4 - step)}
            for k in (1, 3, 2):
                third[o][k].append(send(part, c, k, **row))
    other = links.device(c=1 - pos["c"])
    for part, (a, b, c) in zip(parts, orders):
        src = region(part, **{a: every, b: every})
        planes.append(links.copy(src, src, other))
    for k in (1, 3, 2):
        for o, (part, (a, b, c)) in enumerate(zip(parts, orders)):
            for made in third[o][k]:
                made.wait_recv()
            src = region(part, **{a: every, b: every, c: links.at(c, 4 - k)})
            planes.append(links.copy(src, src, other))
    return planes


def reduce_scatter(links, produce, work, bufs, parts, orders):
    pos, every = links.pos, slice(None)
    natural = ("z", "y", "x")

    def region(part, **index):
        return work.at[index.get("z", every), index.get("y", every), index.get("x", every), pl.ds(*part), :]

    first = [{k: [] for k in (1, 2, 3)} for _ in orders]
    for step in (1, 3, 2, 0):
        z = links.at("z", step)
        produce(z)
        for o, (part, (c, b, a)) in enumerate(zip(parts, orders)):
            got = bufs[o][0]
            if a == "z":
                if step:
                    first[o][step].append(
                        links.copy(region(part, z=z), got.at[step - 1], links.device(z=z))
                    )
                continue
            for k in (1, 3, 2):
                there = links.at(a, k)
                first[o][k].append(
                    links.copy(region(part, **{a: there, "z": z}), got.at[k - 1, z], links.device(**{a: there}))
                )
    second, third = [], []
    for o, (part, (c, b, a)) in enumerate(zip(parts, orders)):
        got, sum1, got2, sum2, got3 = bufs[o]
        for k in (1, 3, 2):
            for made in first[o][k]:
                made.wait_recv()
        left = [n for n in natural if n != a]

        def add(i, _, a=a, left=left, got=got, sum1=sum1, part=part):
            u, v = i // 4, i % 4
            index = {left[0]: u, left[1]: v, a: pos[a]}
            total = work[index["z"], index["y"], index["x"], pl.ds(*part), :].astype(F32)
            for k in range(3):
                total += got[k, u, v].astype(F32)
            sum1[u, v] = total.astype(BF16)
            return _

        lax.fori_loop(0, 16, add, 0)
        lead = left.index(b) == 0
        made2 = []
        for k in (1, 3, 2):
            there = links.at(b, k)
            src = sum1.at[there] if lead else sum1.at[:, there]
            made2.append(links.copy(src, got2.at[k - 1], links.device(**{b: there})))
        second.append(made2)
    for o, (part, (c, b, a)) in enumerate(zip(parts, orders)):
        got, sum1, got2, sum2, got3 = bufs[o]
        for made in second[o]:
            made.wait_recv()
        left = [n for n in natural if n != a]
        lead = left.index(b) == 0

        def add2(v, _, sum1=sum1, sum2=sum2, got2=got2, lead=lead, b=b):
            total = (sum1[pos[b], v] if lead else sum1[v, pos[b]]).astype(F32)
            for k in range(3):
                total += got2[k, v].astype(F32)
            sum2[v] = total.astype(BF16)
            return _

        lax.fori_loop(0, 4, add2, 0)
        made3 = []
        for k in (1, 3, 2):
            there = links.at(c, k)
            made3.append(links.copy(sum2.at[there], got3.at[k - 1], links.device(**{c: there})))
        third.append(made3)
    totals = []
    for o, (part, (c, b, a)) in enumerate(zip(parts, orders)):
        got, sum1, got2, sum2, got3 = bufs[o]
        for made in third[o]:
            made.wait_recv()
        total = sum2[pos[c]].astype(F32)
        for k in range(3):
            total += got3[k].astype(F32)
        totals.append(total)
    return totals


def factor_steps(work, first, last):
    lane = lax.broadcasted_iota(jnp.int32, (8, 128), 1)
    row = lax.broadcasted_iota(jnp.int32, (8, 1), 0)

    def panel_step(p, _):
        start = pl.multiple_of(p * 8, 8)
        panel = work[pl.ds(start, 8), :]
        left = panel[:, :128]
        cols = [jnp.sum(jnp.where(lane == start + k, left, 0.0), axis=1, keepdims=True) for k in range(8)]
        scale = jnp.zeros((8, 1), F32)
        for k in range(8):
            pivot = cols[k][k : k + 1]
            scale = jnp.where(row == k, pivot, scale)
            below = jnp.where(row > k, cols[k] / pivot, 0.0)
            panel = panel - below * panel[k : k + 1]
            for m in range(k + 1, 8):
                cols[m] = cols[m] - below * cols[m][k : k + 1]
        panel = panel / jnp.sqrt(scale)
        work[pl.ds(start, 8), :] = panel
        rest = jnp.where(lane >= start + 8, panel[:, :128], 0.0)
        work[...] = work[...] - dot(rest, panel, (((0,), (0,)), ((), ())), HIGHEST)
        return _

    lax.fori_loop(first, last, panel_step, 0)


def kernel(stop, act, start, new_ref, sketch_ref, a_v, s_all, t_all, out_d, in_d, work, fac, proj_t,
           h_all, h_in, h_mid, h_out, *rest):
    bufs = [rest[5 * o : 5 * o + 5] for o in range(3)]
    local_sem, send_sems, recv_sems = rest[15:]
    links = Links(send_sems, recv_sems)
    pos = links.pos
    c, z, y, x = pos["c"], pos["z"], pos["y"], pos["x"]
    chunk = 4096

    load_s = pltpu.make_async_copy(start, s_all.at[c, z, y, x], local_sem.at[8])
    load_s.start()
    loads = []
    for i in range(8):
        cols = pl.ds(i * chunk, chunk)
        loads.append(pltpu.make_async_copy(act.at[:, cols], a_v.at[:, cols], local_sem.at[i]))
        loads[-1].start()

    barrier = pltpu.get_barrier_semaphore()
    mates = [(lax.rem(links.seq + k, 8), links.dp) for k in range(1, 8)]
    plane = [(links.seq, lax.rem(links.dp + k, 16)) for k in range(1, 16)]
    for device in mates + plane:
        pl.semaphore_signal(barrier, 1, device_id=device, device_id_type=MESH)
    pl.semaphore_wait(barrier, len(mates) + len(plane))

    load_s.wait()
    planes = gather(links, s_all, START_PARTS, ORDERS)
    for load in loads:
        load.wait()

    def project(colour):
        def body(i, total):
            cols = pl.ds(pl.multiple_of((i * 2 + colour) * chunk, chunk), chunk)
            return total + dot(a_v[:, cols], s_all[colour, i].reshape(chunk, 128))
        return body

    total = lax.fori_loop(0, 4, project(c), jnp.zeros((256, 128), F32))
    for made in planes:
        made.wait_recv()
    total = lax.fori_loop(0, 4, project(1 - c), total)
    proj_t[...] = total.T.astype(BF16)
    if stop == 1:
        links.drain()
        new_ref[...] = total.astype(BF16)
        sketch_ref[...] = total
        return

    def block(colour, zz, yx):
        cols = pl.ds(pl.multiple_of((zz * 32 + colour * 16 + yx) * 256, 256), 256)
        return dot(proj_t[...], a_v[:, cols])

    pair = []
    for step in (1, 3, 2, 0):
        zz = links.at("z", step)

        def give(i, _, zz=zz):
            out_d[zz, i // 4, i % 4] = block(1 - c, zz, i).astype(BF16)
            return _

        lax.fori_loop(0, 16, give, 0)
        pair.append(links.copy(out_d.at[zz], in_d.at[zz], links.device(c=1 - c)))

    waiting = iter(pair)

    def produce(zz):
        next(waiting).wait_recv()

        def own(i, _):
            u, v = i // 4, i % 4
            work[zz, u, v] = (block(c, zz, i) + in_d[zz, u, v].astype(F32)).astype(BF16)
            return _

        lax.fori_loop(0, 16, own, 0)

    totals = reduce_scatter(links, produce, work, bufs, PANEL_PARTS, ORDERS)
    pulled_t = jnp.concatenate(totals, axis=0)
    if stop == 2:
        links.drain()
        new_ref[...] = pulled_t.T.astype(BF16)
        sketch_ref[...] = pulled_t.T
        return
    t_all[c, z, y, x] = pulled_t.astype(BF16)
    planes = gather(links, t_all, PANEL_PARTS, ORDERS)

    NT = (((1,), (1,)), ((), ()))

    def gather_sums(colour):
        def body(i, sums):
            raw, gram = sums
            for u in range(4):
                piece = t_all[colour, i // 4, i % 4, u]
                cols = pl.ds(pl.multiple_of(((i // 4) * 32 + colour * 16 + (i % 4) * 4 + u) * 256, 256), 256)
                raw = raw + dot(a_v[:, cols], piece, NT)
                gram = gram + dot(piece, piece, NT)
            return raw, gram
        return body

    sums = (jnp.zeros((256, 128), F32), jnp.zeros((128, 128), F32))
    sums = lax.fori_loop(0, 16, gather_sums(c), sums)
    for made in planes:
        made.wait_recv()
    raw, gram = lax.fori_loop(0, 16, gather_sums(1 - c), sums)

    rows = lax.broadcasted_iota(jnp.int32, (128, 128), 0)
    cols = lax.broadcasted_iota(jnp.int32, (128, 128), 1)
    eye = rows == cols
    diagonal = jnp.where(eye, gram, 0.0)
    d_row = 1.0 / jnp.sqrt(jnp.sum(diagonal, axis=0, keepdims=True))
    d_col = 1.0 / jnp.sqrt(jnp.sum(diagonal, axis=1, keepdims=True))
    fac[:, :128] = gram * d_row * d_col
    fac[:, 128:] = jnp.where(eye, 1.0, 0.0).astype(F32)
    raw = raw * d_row
    h_all[...] = dot(raw, raw, (((0,), (0,)), ((), ())), HIGHEST)

    seq = links.seq
    made = []
    for k in range(1, 8):
        s = lax.rem(seq + k, 8)
        made.append(links.copy(h_all.at[pl.ds(pl.multiple_of(s * 16, 16), 16)], h_in.at[k - 1], (s, links.dp)))
    factor_steps(fac, 0, 5)
    mine = h_all[pl.ds(pl.multiple_of(seq * 16, 16), 16)]
    for k in range(7):
        made[k].wait_recv()
        mine += h_in[k]
    h_mid[0] = mine
    made = []
    for k in range(1, 16):
        made.append(links.copy(h_mid.at[0], h_mid.at[k], (seq, lax.rem(links.dp + k, 16))))
    factor_steps(fac, 5, 11)
    for m in made:
        m.wait_recv()
    mine = jnp.sum(h_mid[...], axis=0)
    here = pl.ds(pl.multiple_of(seq * 16, 16), 16)
    h_out[here] = mine
    made = []
    for k in range(1, 8):
        made.append(links.copy(h_out.at[here], h_out.at[here], (lax.rem(seq + k, 8), links.dp)))
    factor_steps(fac, 11, 16)
    inverse = fac[:, 128:]
    panel = dot(inverse, pulled_t * d_col, precision=HIGHEST).T.astype(BF16)
    new_ref[...] = panel
    for m in made:
        m.wait_recv()
    ritz = dot(dot(inverse, h_out[...], precision=HIGHEST), inverse, NT, HIGHEST)

    mean = jnp.sum(jnp.where(eye, ritz, 0.0)) / 128
    shifted = ritz - jnp.where(eye, mean, 0.0)
    sign = shifted / (jnp.sqrt(jnp.sum(shifted * shifted)) + 1e-6)

    def sweep(_, sign):
        square = dot(sign, sign, precision=HIGHEST)
        return 0.5 * (3.0 * sign - dot(square, sign, precision=HIGHEST))

    sign = lax.fori_loop(0, NS_STEPS, sweep, sign)
    positive = 0.5 * (shifted + dot(shifted, sign, precision=HIGHEST))
    sketch_ref[...] = math.sqrt(32768) / mean * dot(panel.astype(F32), positive, precision=HIGHEST)
    links.drain()


def local(stop, activations, start_panel):
    scratch = [
        pltpu.VMEM((256, 32768), BF16),
        pltpu.VMEM((2, 4, 4, 4, 256, 128), BF16),
        pltpu.VMEM((2, 4, 4, 4, 128, 256), BF16),
        pltpu.VMEM((4, 4, 4, 128, 256), BF16),
        pltpu.VMEM((4, 4, 4, 128, 256), BF16),
        pltpu.VMEM((4, 4, 4, 128, 256), BF16),
        pltpu.VMEM((128, 256), F32),
        pltpu.VMEM((128, 256), BF16),
        pltpu.VMEM((128, 128), F32),
        pltpu.VMEM((7, 16, 128), F32),
        pltpu.VMEM((16, 16, 128), F32),
        pltpu.VMEM((128, 128), F32),
    ]
    for _, rows in PANEL_PARTS:
        scratch += [
            pltpu.VMEM((3, 4, 4, rows, 256), BF16),
            pltpu.VMEM((4, 4, rows, 256), BF16),
            pltpu.VMEM((3, 4, rows, 256), BF16),
            pltpu.VMEM((4, rows, 256), BF16),
            pltpu.VMEM((3, rows, 256), BF16),
        ]
    scratch += [
        pltpu.SemaphoreType.DMA((9,)),
        pltpu.SemaphoreType.DMA((N_SEMS,)),
        pltpu.SemaphoreType.DMA((N_SEMS,)),
    ]
    return pl.pallas_call(
        functools.partial(kernel, stop),
        out_shape=(
            jax.ShapeDtypeStruct((256, 128), BF16),
            jax.ShapeDtypeStruct((256, 128), F32),
        ),
        in_specs=[pl.BlockSpec(memory_space=pl.ANY)] * 2,
        out_specs=(pl.BlockSpec(memory_space=pltpu.VMEM),) * 2,
        scratch_shapes=scratch,
        compiler_params=pltpu.CompilerParams(
            collective_id=0, has_side_effects=True, vmem_limit_bytes=60 << 20
        ),
        name="subspace",
    )(activations, start_panel)


def solution(mesh, stop=0):
    spec = P(("seq", "dp"), None)
    return jax.shard_map(
        functools.partial(local, stop), mesh=mesh, in_specs=(spec, spec), out_specs=(spec, spec), check_vma=False
    )
```

time: 1180 us -> 155 us (0.13)
  waiting for transfers between devices: 1090 us -> 0 us
  Pallas kernels: 0 us -> 151 us
  matrix products: 48 us -> 0 us
  other arithmetic: 26.6 us -> 0 us
  between operations: 15.4 us -> 0.64 us
    reduce_scatter x1 -> x0, waiting for transfers between devices: 641 us -> none  [local(): lax.psum_scatter(lax.dot_general(activations, projected, (((0,), (0,)), (...]
    psum x2 -> x0, waiting for transfers between devices: 302 us -> none  [the longest x1 167 us: local(): cross_gram = lax.psum(local_gram, ('seq', 'dp'))]
    pallas_call x0 -> x1, Pallas kernels: none -> 151 us  [local(): pl.pallas_call(functools.partial(kernel, stop), out_shape=(jax.ShapeDtype...]
    all_gather x2 -> x0, waiting for transfers between devices: 144 us -> none  [the longest x1 77 us: local(): lax.all_gather(start_panel, ('seq', 'dp'), axis=0, tiled=True)]
    dot_general x31 -> x0, matrix products: 46.1 us -> none  [the longest x2 26.5 us: add_block(): return jnp.dot(activations, piece, preferred_element_type=jnp.float32)]
    another operation x5 -> x0, other arithmetic: 22.9 us -> none  [the longest x3 12.4 us: orthonormal(): factor_low = jnp.linalg.cholesky(cross_gram)]
  transfers between devices with their start and end apart: 5 -> 0, of which waited for: 5 -> 0; matrix products, arithmetic and copies ran while one was open for 0% -> 0% of each run, Pallas kernels for 0% -> 0%
where the time goes in v1:
time: 155 us
  Pallas kernels  151 us (97%)
  local copies, waits for them, and re-layouts  3.04 us (2%)
    pallas_call x1, Pallas kernels, local(): pl.pallas_call(functools.partial(kernel, stop), out_shape=(jax.ShapeDtype...  151 us

profile of v1, /device:TPU:1, one launch (start us, length us, event | category | flops | bytes accessed | tf_op | source)
XLA Modules:
  0.0 155.1 jit_solution(16595919444383510568)
XLA Ops:
  0.6 151.4 %subspace.1 = (bf16[256,128]{1,0:T(8,128)(2,1)}, f32[256,128]{1,0:T(8,128)}) custom-call(bf16[256,32768]{1,0:T(8,128)(2,1)} %act.1, bf16[256,128]{1,0:T(8,128)(2,1)} %start.1), custom_call_target="tpu_custom_call" | custom-call | tf_op jit(solution)/shard_map/subspace/pallas_call | solution.py:394
  152.0 1.5 copy.6
  153.5 1.6 %copy.7 = f32[256,128]{1,0:T(8,128)} copy(f32[256,128]{1,0:T(8,128)} %get-tuple-element.5) | data formatting | bytes 262144

commit v2 on v0

v2 whole, which is shorter than its diff:
```python
import math

import jax
import jax.numpy as jnp
from jax import lax
from jax.experimental import pallas as pl
from jax.experimental.pallas import tpu as pltpu
from jax.sharding import PartitionSpec as P

NS_STEPS = 12
MESH = pl.DeviceIdType.MESH
F32, BF16 = jnp.float32, jnp.bfloat16
HIGHEST = lax.Precision.HIGHEST
ORDERS = (("x", "y", "z"), ("z", "x", "y"), ("y", "z", "x"))
START_PARTS = ((0, 96), (96, 80), (176, 80))
PANEL_PARTS = (((0, 48), (48, 32), (80, 48)), ((0, 32), (32, 48), (80, 48)))
N_SEMS = 3 * 42 + 2 * 24 + 5 + 6


def dot(a, b, dims=(((1,), (0,)), ((), ())), precision=None):
    return lax.dot_general(a, b, dims, precision=precision, preferred_element_type=F32)


class Links:
    def __init__(self, sems):
        seq, dp = lax.axis_index("seq"), lax.axis_index("dp")
        self.pos = dict(z=seq // 2, c=seq % 2, y=dp // 4, x=dp % 4)
        self.seq, self.dp = seq, dp
        self.sems, self.used, self.sent = sems, 0, []

    def sem(self):
        self.used += 1
        return self.used - 1

    def at(self, axis, step):
        return lax.rem(self.pos[axis] + step, 4)

    def device(self, **other):
        p = {**self.pos, **other}
        return (p["z"] * 2 + p["c"], p["y"] * 4 + p["x"])

    def copy(self, src, dst, device, send, recv):
        pltpu.make_async_remote_copy(
            src_ref=src,
            dst_ref=dst,
            send_sem=self.sems.at[send],
            recv_sem=self.sems.at[recv],
            device_id=device,
            device_id_type=MESH,
        ).start()

    def wait(self, sem, like):
        pltpu.make_async_copy(like, like, self.sems.at[sem]).wait()

    def drain(self):
        for sem, like in self.sent:
            self.wait(sem, like)


def gather(links, buf, parts, orders, handed, half=()):
    pos, every, three, two = links.pos, slice(None), pl.ds(0, 3), pl.ds(0, 2)
    halves = {1: pl.ds(0, 2), 3: pl.ds(2, 2)}
    other = links.device(c=1 - pos["c"])
    each = list(enumerate(zip(parts, orders)))

    def region(part, **index):
        p = {**pos, **index}
        return buf.at[(p["c"], p["z"], p["y"], p["x"], *half, pl.ds(*part), slice(None))]

    sends = [[links.sem() for _ in range(5)] for _ in orders]
    gets = [[links.sem() for _ in range(9)] for _ in orders]
    for o, (part, (a, b, c)) in each:
        sizes = ({a: three}, {a: every, b: three}, {a: every, b: every, c: two}, {a: every, b: every}, {a: every, b: every, c: every})
        links.sent += [(sem, region(part, **size)) for sem, size in zip(sends[o], sizes)]
        handed.append((gets[o][8], region(part, **sizes[4])))
    rows = [[] for _ in orders]

    def send(o, kind, get, axis, step, **index):
        src = region(parts[o], **index)
        links.copy(src, src, links.device(**{axis: links.at(axis, step)}), sends[o][kind], gets[o][get])

    def wait(o, get, **size):
        links.wait(gets[o][get], region(parts[o], **size))

    def spread(o, row):
        a, b, c = orders[o]
        rows[o].append(row)
        for k in (1, 3):
            send(o, 2, 2 + len(rows[o]), c, k, **row)

    def forward(o, j):
        a, b, c = orders[o]
        wait(o, 3 + j, **{a: every, c: two})
        for k in (1, 3):
            send(o, 3, 7, c, k, **{**rows[o][j], a: halves[k], c: links.at(c, 4 - k)})

    def hand(o, **index):
        a, b, c = orders[o]
        src = region(parts[o], **{a: every, b: every, **index})
        links.copy(src, src, other, sends[o][4], gets[o][8])

    for o, (part, (a, b, c)) in each:
        for k in (1, 3, 2):
            send(o, 0, 0, a, k)
    yield
    for o, (part, (a, b, c)) in each:
        wait(o, 0, **{a: three})
        for k in (1, 3, 2):
            send(o, 1, 2 if k == 2 else 1, b, k, **{a: every})
        spread(o, {a: every})
    yield
    for o, (part, (a, b, c)) in each:
        wait(o, 1, **{a: every, b: two})
        for step in (1, 3):
            spread(o, {a: every, b: links.at(b, 4 - step)})
    yield
    for o, _ in each:
        forward(o, 0)
    for o, (part, (a, b, c)) in each:
        wait(o, 2, **{a: every})
        spread(o, {a: every, b: links.at(b, 2)})
        hand(o)
    yield
    for j in (1, 2, 3):
        for o, _ in each:
            forward(o, j)
    for k in (1, 3):
        for o, (part, (a, b, c)) in each:
            hand(o, **{c: links.at(c, 4 - k)})
    yield
    for o, (part, (a, b, c)) in each:
        wait(o, 7, **{a: every, b: every})
        hand(o, **{c: links.at(c, 2)})


class Reduce:
    natural = ("z", "y", "x")
    steps = (2, 1, 3, 0)
    halves = {1: pl.ds(0, 2), 3: pl.ds(2, 2)}

    def __init__(self, links, work, h, bufs, parts, orders):
        self.links, self.work, self.h, self.bufs = links, work, h, bufs
        self.parts, self.orders = parts, orders
        self.each = list(enumerate(zip(parts, orders)))
        self.sends = [[links.sem() for _ in range(4)] for _ in orders]
        self.gets = [[links.sem() for _ in range(4)] for _ in orders]
        two, three = pl.ds(0, 2), pl.ds(0, 3)
        self.sizes = []
        for o, (part, (c, b, a)) in self.each:
            sum1, sum2 = bufs[o][2], bufs[o][4]
            likes = (self.region(part, **{a: 0}), self.region(part, **{a: two}), sum1.at[three], sum2.at[three])
            links.sent += list(zip(self.sends[o], likes))
            self.sizes.append(likes)

    def at(self, part, **index):
        every = slice(None)
        where = [index.get(n, every) for n in self.natural]
        return (*where, self.h, pl.ds(*part), every)

    def region(self, part, **index):
        return self.work.at[self.at(part, **index)]

    def send(self, o, kind, src, dst, axis, to):
        links = self.links
        links.copy(src, dst, links.device(**{axis: to}), self.sends[o][kind], self.gets[o][kind])

    def wait(self, o, kind):
        self.links.wait(self.gets[o][kind], self.sizes[o][kind])

    def start(self, n=None):
        links = self.links
        for o, (part, (c, b, a)) in self.each:
            via = self.bufs[o][0]
            left = "x" if a == "y" else "y"
            if a == "z" and n not in (None, 0):
                continue
            for i, k in enumerate((1, 3)):
                index, dst = {a: links.at(a, 2), left: self.halves[k]}, via.at[i]
                if a != "z" and n is not None:
                    z = links.at("z", self.steps[n])
                    index["z"], dst = z, via.at[i, z]
                self.send(o, 0, self.region(part, **index), dst, a, links.at(a, k))

    def forward(self):
        links, work = self.links, self.work
        for o, (part, (c, b, a)) in self.each:
            via, got = self.bufs[o][:2]
            self.wait(o, 0)
            for i, k in enumerate((1, 3)):
                there = links.at(a, k)
                for u in range(4):
                    for j in range(2):
                        v = 2 * i + j
                        if a == "z":
                            block, piece = dict(z=there, y=v, x=u), via[i, j, u]
                        elif a == "y":
                            block, piece = dict(z=u, y=there, x=v), via[i, u, j]
                        else:
                            block, piece = dict(z=u, y=v, x=there), via[i, u, j]
                        where = self.at(part, **block)
                        work[where] = (work[where].astype(F32) + piece.astype(F32)).astype(BF16)
                self.send(o, 1, self.region(part, **{a: there}), got.at[i], a, there)

    def own(self):
        links, pos = self.links, self.links.pos
        for o, (part, (c, b, a)) in self.each:
            got, sum1, got2 = self.bufs[o][1:4]
            self.wait(o, 1)
            left = [n for n in self.natural if n != a]
            lead = left.index(b) == 0
            for step in (2, 1, 3, 0):
                there = links.at(b, step)
                for w in range(4):
                    u, v = (there, w) if lead else (w, there)
                    mine = self.work[self.at(part, **{a: pos[a], left[0]: u, left[1]: v})].astype(F32)
                    sum1[u, v] = (mine + got[0, u, v].astype(F32) + got[1, u, v].astype(F32)).astype(BF16)
                if step:
                    src = sum1.at[there] if lead else sum1.at[:, there]
                    self.send(o, 2, src, got2.at[step - 1], b, there)

    def last_axis(self):
        links, pos = self.links, self.links.pos
        for o, (part, (c, b, a)) in self.each:
            sum1, got2, sum2, got3 = self.bufs[o][2:]
            self.wait(o, 2)
            lead = [n for n in self.natural if n != a].index(b) == 0
            for step in (2, 1, 3, 0):
                v = links.at(c, step)
                total = (sum1[pos[b], v] if lead else sum1[v, pos[b]]).astype(F32)
                for k in range(3):
                    total += got2[k, v].astype(F32)
                sum2[v] = total.astype(BF16)
                if step:
                    self.send(o, 3, sum2.at[v], got3.at[step - 1], c, v)

    def finish(self):
        totals = []
        for o, (part, (c, b, a)) in self.each:
            sum2, got3 = self.bufs[o][4:]
            self.wait(o, 3)
            total = sum2[self.links.pos[c]].astype(F32)
            for k in range(3):
                total += got3[k].astype(F32)
            totals.append(total)
        return jnp.concatenate(totals, axis=0)


def factor_steps(work, first, last):
    lane = lax.broadcasted_iota(jnp.int32, (8, 128), 1)
    row = lax.broadcasted_iota(jnp.int32, (8, 1), 0)

    def panel_step(p, _):
        start = pl.multiple_of(p * 8, 8)
        panel = work[pl.ds(start, 8), :]
        left = panel[:, :128]
        cols = [jnp.sum(jnp.where(lane == start + k, left, 0.0), axis=1, keepdims=True) for k in range(8)]
        scale = jnp.zeros((8, 1), F32)
        for k in range(8):
            pivot = cols[k][k : k + 1]
            scale = jnp.where(row == k, pivot, scale)
            below = jnp.where(row > k, cols[k] / pivot, 0.0)
            panel = panel - below * panel[k : k + 1]
            for m in range(k + 1, 8):
                cols[m] = cols[m] - below * cols[m][k : k + 1]
        panel = panel / jnp.sqrt(scale)
        work[pl.ds(start, 8), :] = panel
        rest = jnp.where(lane >= start + 8, panel[:, :128], 0.0)
        work[...] = work[...] - dot(rest, panel, (((0,), (0,)), ((), ())), HIGHEST)
        return _

    lax.fori_loop(first, last, panel_step, 0)


def kernel(act, start, new_ref, sketch_ref, a_v, s_all, t_all, out_d, in_d, work, fac, proj_t,
           h_all, h_in, h_mid, h_out, *rest):
    bufs = [[rest[18 * h + 6 * o : 18 * h + 6 * o + 6] for o in range(3)] for h in range(2)]
    local_sem, sems = rest[36:]
    links = Links(sems)
    pos = links.pos
    c, z, y, x = pos["c"], pos["z"], pos["y"], pos["x"]
    chunk = 4096

    load_s = pltpu.make_async_copy(start, s_all.at[c, z, y, x], local_sem.at[8])
    load_s.start()
    loads = []
    for i in range(8):
        cols = pl.ds(i * chunk, chunk)
        loads.append(pltpu.make_async_copy(act.at[:, cols], a_v.at[:, cols], local_sem.at[i]))
        loads[-1].start()

    barrier = pltpu.get_barrier_semaphore()
    near = [links.device(**{axis: links.at(axis, k)}) for axis in ("x", "y", "z") for k in (1, 2, 3)]
    near.append(links.device(c=1 - c))
    for device in near:
        pl.semaphore_signal(barrier, 1, device_id=device, device_id_type=MESH)
    pl.semaphore_wait(barrier, len(near))

    load_s.wait()
    handed = []
    for _ in gather(links, s_all, START_PARTS, ORDERS, handed):
        pass
    for load in loads:
        load.wait()

    def project(colour):
        def body(i, total):
            cols = pl.ds(pl.multiple_of((i * 2 + colour) * chunk, chunk), chunk)
            return total + dot(a_v[:, cols], s_all[colour, i].reshape(chunk, 128))
        return body

    total = lax.fori_loop(0, 4, project(c), jnp.zeros((256, 128), F32))
    for sem, like in handed:
        links.wait(sem, like)
    total = lax.fori_loop(0, 4, project(1 - c), total)
    proj_t[...] = total.T.astype(BF16)

    def block(colour, zz, yx):
        cols = pl.ds(pl.multiple_of((zz * 32 + colour * 16 + yx) * 256, 256), 256)
        return dot(proj_t[...], a_v[:, cols])

    pair = [links.sem() for _ in range(4)]
    pair_sent = links.sem()
    links.sent.append((pair_sent, out_d))
    order = [links.at("z", step) for step in (2, 1, 3, 0)]
    given = []

    def give():
        zz = order[len(given)]
        for i in range(16):
            piece = block(1 - c, zz, i).astype(BF16)
            for h in range(2):
                out_d[zz, i // 4, i % 4, h] = piece[:, h * 128 : h * 128 + 128]
        links.copy(out_d.at[zz], in_d.at[zz], links.device(c=1 - c), pair_sent, pair[len(given)])
        given.append(zz)

    def produce(n):
        while len(given) < min(n + 2, 4):
            give()
        zz = order[n]
        links.wait(pair[n], in_d.at[zz])
        for i in range(16):
            u, v = i // 4, i % 4
            piece = block(c, zz, i)
            for h in range(2):
                mine = piece[:, h * 128 : h * 128 + 128] + in_d[zz, u, v, h].astype(F32)
                work[zz, u, v, h] = mine.astype(BF16)

    handed, pulled_t, gathers = [], [None, None], [None, None]
    sums = [Reduce(links, work, h, bufs[h], PANEL_PARTS[h], ORDERS) for h in range(2)]

    def done(h):
        pulled_t[h] = sums[h].finish()
        t_all[c, z, y, x, h] = pulled_t[h].astype(BF16)
        gathers[h] = gather(links, t_all, PANEL_PARTS[h], ORDERS, handed, (h,))
        next(gathers[h])

    for n in range(4):
        produce(n)
        sums[0].start(n)
    sums[1].start()
    sums[0].forward()
    sums[1].forward()
    sums[0].own()
    sums[1].own()
    sums[0].last_axis()
    sums[1].last_axis()
    done(0)
    done(1)
    next(gathers[0])
    next(gathers[1])
    next(gathers[0])
    next(gathers[1])
    next(gathers[0])
    next(gathers[1])
    for _ in gathers[0]:
        pass
    for _ in gathers[1]:
        pass
    pulled_t = jnp.concatenate(pulled_t, axis=1)

    NT = (((1,), (1,)), ((), ()))

    def gather_sums(colour):
        def body(i, sums):
            raw, gram = sums
            for u in range(16):
                piece = jnp.concatenate([t_all[colour, i, u // 4, u % 4, h] for h in range(2)], axis=1)
                cols = pl.ds(pl.multiple_of((i * 32 + colour * 16 + u) * 256, 256), 256)
                raw = raw + dot(a_v[:, cols], piece, NT)
                gram = gram + dot(piece, piece, NT)
            return raw, gram
        return body

    sums = (jnp.zeros((256, 128), F32), jnp.zeros((128, 128), F32))
    sums = lax.fori_loop(0, 4, gather_sums(c), sums)
    for sem, like in handed:
        links.wait(sem, like)
    raw, gram = lax.fori_loop(0, 4, gather_sums(1 - c), sums)

    rows = lax.broadcasted_iota(jnp.int32, (128, 128), 0)
    cols = lax.broadcasted_iota(jnp.int32, (128, 128), 1)
    eye = rows == cols
    diagonal = jnp.where(eye, gram, 0.0)
    d_row = 1.0 / jnp.sqrt(jnp.sum(diagonal, axis=0, keepdims=True))
    d_col = 1.0 / jnp.sqrt(jnp.sum(diagonal, axis=1, keepdims=True))
    fac[:, :128] = gram * d_row * d_col
    fac[:, 128:] = jnp.where(eye, 1.0, 0.0).astype(F32)
    raw = raw * d_row
    h_all[...] = dot(raw, raw, (((0,), (0,)), ((), ())), HIGHEST)

    seq, dp = links.seq, links.dp
    here = pl.ds(pl.multiple_of(seq * 16, 16), 16)
    sent, got = [links.sem() for _ in range(3)], [links.sem() for _ in range(3)]
    links.sent += [(sent[0], h_in), (sent[1], h_mid.at[pl.ds(1, 15)]), (sent[2], h_in)]
    for k in range(1, 8):
        s = lax.rem(seq + k, 8)
        src = h_all.at[pl.ds(pl.multiple_of(s * 16, 16), 16)]
        links.copy(src, h_in.at[k - 1], (s, dp), sent[0], got[0])
    factor_steps(fac, 0, 5)
    links.wait(got[0], h_in)
    h_mid[0] = h_all[here] + jnp.sum(h_in[...], axis=0)
    for k in range(1, 16):
        links.copy(h_mid.at[0], h_mid.at[k], (seq, lax.rem(dp + k, 16)), sent[1], got[1])
    factor_steps(fac, 5, 11)
    links.wait(got[1], h_mid.at[pl.ds(1, 15)])
    h_out[here] = jnp.sum(h_mid[...], axis=0)
    for k in range(1, 8):
        links.copy(h_out.at[here], h_out.at[here], (lax.rem(seq + k, 8), dp), sent[2], got[2])
    factor_steps(fac, 11, 16)
    inverse = fac[:, 128:]
    panel = dot(inverse, pulled_t * d_col, precision=HIGHEST).T.astype(BF16)
    new_ref[...] = panel
    links.wait(got[2], h_in)
    ritz = dot(dot(inverse, h_out[...], precision=HIGHEST), inverse, NT, HIGHEST)

    mean = jnp.sum(jnp.where(eye, ritz, 0.0)) / 128
    shifted = ritz - jnp.where(eye, mean, 0.0)
    sign = shifted / (jnp.sqrt(jnp.sum(shifted * shifted)) + 1e-6)

    def sweep(_, sign):
        square = dot(sign, sign, precision=HIGHEST)
        return 0.5 * (3.0 * sign - dot(square, sign, precision=HIGHEST))

    sign = lax.fori_loop(0, NS_STEPS, sweep, sign)
    positive = 0.5 * (shifted + dot(shifted, sign, precision=HIGHEST))
    sketch_ref[...] = math.sqrt(32768) / mean * dot(panel.astype(F32), positive, precision=HIGHEST)
    links.drain()


def local(activations, start_panel):
    scratch = [
        pltpu.VMEM((256, 32768), BF16),
        pltpu.VMEM((2, 4, 4, 4, 256, 128), BF16),
        pltpu.VMEM((2, 4, 4, 4, 2, 128, 128), BF16),
        pltpu.VMEM((4, 4, 4, 2, 128, 128), BF16),
        pltpu.VMEM((4, 4, 4, 2, 128, 128), BF16),
        pltpu.VMEM((4, 4, 4, 2, 128, 128), BF16),
        pltpu.VMEM((128, 256), F32),
        pltpu.VMEM((128, 256), BF16),
        pltpu.VMEM((128, 128), F32),
        pltpu.VMEM((7, 16, 128), F32),
        pltpu.VMEM((16, 16, 128), F32),
        pltpu.VMEM((128, 128), F32),
    ]
    for parts in PANEL_PARTS:
        for (_, rows), order in zip(parts, ORDERS):
            along_z = order[2] == "z"
            scratch += [
                pltpu.VMEM((2, 2, 4, rows, 128) if along_z else (2, 4, 2, rows, 128), BF16),
                pltpu.VMEM((2, 4, 4, rows, 128), BF16),
                pltpu.VMEM((4, 4, rows, 128), BF16),
                pltpu.VMEM((3, 4, rows, 128), BF16),
                pltpu.VMEM((4, rows, 128), BF16),
                pltpu.VMEM((3, rows, 128), BF16),
            ]
    scratch += [
        pltpu.SemaphoreType.DMA((9,)),
        pltpu.SemaphoreType.DMA((N_SEMS,)),
    ]
    return pl.pallas_call(
        kernel,
        out_shape=(
            jax.ShapeDtypeStruct((256, 128), BF16),
            jax.ShapeDtypeStruct((256, 128), F32),
        ),
        in_specs=[pl.BlockSpec(memory_space=pl.ANY)] * 2,
        out_specs=(pl.BlockSpec(memory_space=pltpu.VMEM),) * 2,
        scratch_shapes=scratch,
        compiler_params=pltpu.CompilerParams(
            collective_id=0, has_side_effects=True, vmem_limit_bytes=60 << 20
        ),
        name="subspace",
    )(activations, start_panel)


def solution(mesh):
    spec = P(("seq", "dp"), None)
    return jax.shard_map(
        local, mesh=mesh, in_specs=(spec, spec), out_specs=(spec, spec), check_vma=False
    )
```

time: 1180 us -> 123 us (0.10)
  waiting for transfers between devices: 1090 us -> 0 us
  Pallas kernels: 0 us -> 120 us
  matrix products: 48 us -> 0 us
  other arithmetic: 26.6 us -> 0 us
  between operations: 15.4 us -> 0.64 us
    reduce_scatter x1 -> x0, waiting for transfers between devices: 641 us -> none  [local(): lax.psum_scatter(lax.dot_general(activations, projected, (((0,), (0,)), (...]
    psum x2 -> x0, waiting for transfers between devices: 302 us -> none  [the longest x1 167 us: local(): cross_gram = lax.psum(local_gram, ('seq', 'dp'))]
    all_gather x2 -> x0, waiting for transfers between devices: 144 us -> none  [the longest x1 77 us: local(): lax.all_gather(start_panel, ('seq', 'dp'), axis=0, tiled=True)]
    pallas_call x0 -> x1, Pallas kernels: none -> 120 us  [local(): pl.pallas_call(kernel, out_shape=(jax.ShapeDtypeStruct((256, 128), BF16),...]
    dot_general x31 -> x0, matrix products: 46.1 us -> none  [the longest x2 26.5 us: add_block(): return jnp.dot(activations, piece, preferred_element_type=jnp.float32)]
    another operation x5 -> x0, other arithmetic: 22.9 us -> none  [the longest x3 12.4 us: orthonormal(): factor_low = jnp.linalg.cholesky(cross_gram)]
  transfers between devices with their start and end apart: 5 -> 0, of which waited for: 5 -> 0; matrix products, arithmetic and copies ran while one was open for 0% -> 0% of each run, Pallas kernels for 0% -> 0%
where the time goes in v2:
time: 123 us
  Pallas kernels  120 us (98%)
  local copies, waits for them, and re-layouts  3.04 us (2%)
    pallas_call x1, Pallas kernels, local(): pl.pallas_call(kernel, out_shape=(jax.ShapeDtypeStruct((256, 128), BF16),...  120 us
    unnamed x2, local copies, waits for them, and re-layouts  3.04 us

profile of v2, /device:TPU:1, one launch (start us, length us, event | category | flops | bytes accessed | tf_op | source)
XLA Modules:
  0.0 123.3 jit_solution(10132551269998138928)
XLA Ops:
  0.6 119.6 %subspace.1 = (bf16[256,128]{1,0:T(8,128)(2,1)}, f32[256,128]{1,0:T(8,128)}) custom-call(bf16[256,32768]{1,0:T(8,128)(2,1)} %act.1, bf16[256,128]{1,0:T(8,128)(2,1)} %start.1), custom_call_target="tpu_custom_call" | custom-call | tf_op jit(solution)/shard_map/subspace/pallas_call | solution.py:480
  120.3 1.5 %copy.6 = bf16[256,128]{1,0:T(8,128)(2,1)} copy(bf16[256,128]{1,0:T(8,128)(2,1)} %get-tuple-element.4) | data formatting | bytes 131072
  121.7 1.6 %copy.7 = f32[256,128]{1,0:T(8,128)} copy(f32[256,128]{1,0:T(8,128)} %get-tuple-element.5) | data formatting | bytes 262144

commit v3 on v2

--- a/solution.py
+++ b/solution.py
@@ -12,9 +12,8 @@
 F32, BF16 = jnp.float32, jnp.bfloat16
 HIGHEST = lax.Precision.HIGHEST
 ORDERS = (("x", "y", "z"), ("z", "x", "y"), ("y", "z", "x"))
-START_PARTS = ((0, 96), (96, 80), (176, 80))
-PANEL_PARTS = (((0, 48), (48, 32), (80, 48)), ((0, 32), (32, 48), (80, 48)))
-N_SEMS = 3 * 42 + 2 * 24 + 5 + 6
+PARTS = (((0, 48), (48, 32), (80, 48)), ((0, 32), (32, 48), (80, 48)))
+N_SEMS = 4 * 45 + 2 * 24 + 9 + 6
 
 
 def dot(a, b, dims=(((1,), (0,)), ((), ())), precision=None):
@@ -24,7 +23,10 @@
 class Links:
     def __init__(self, sems):
         seq, dp = lax.axis_index("seq"), lax.axis_index("dp")
-        self.pos = dict(z=seq // 2, c=seq % 2, y=dp // 4, x=dp % 4)
+        x, y, z, c = dp % 4, dp // 4, seq // 2, seq % 2
+        first = c == 0
+        self.pos = dict(c=c, x=jnp.where(first, x, y), y=jnp.where(first, y, z), z=jnp.where(first, z, x))
+        self.twin = dict(c=1 - c, x=jnp.where(first, y, x), y=jnp.where(first, z, y), z=jnp.where(first, x, z))
         self.seq, self.dp = seq, dp
         self.sems, self.used, self.sent = sems, 0, []
 
@@ -36,8 +38,21 @@
         return lax.rem(self.pos[axis] + step, 4)
 
     def device(self, **other):
-        p = {**self.pos, **other}
-        return (p["z"] * 2 + p["c"], p["y"] * 4 + p["x"])
+        p, first = {**self.pos, **other}, self.pos["c"] == 0
+        x = jnp.where(first, p["x"], p["z"])
+        y = jnp.where(first, p["y"], p["x"])
+        z = jnp.where(first, p["z"], p["y"])
+        return (z * 2 + p["c"], y * 4 + x)
+
+    def columns(self, colour):
+        first = colour == 0
+        strides = [jnp.where(first, a, b) for a, b in ((32, 1), (4, 32), (1, 4))]
+
+        def columns(*where):
+            place = colour * 16 + sum(i * stride for i, stride in zip(where, strides))
+            return pl.ds(pl.multiple_of(place * 256, 256), 256)
+
+        return columns
 
     def copy(self, src, dst, device, send, recv):
         pltpu.make_async_remote_copy(
@@ -68,11 +83,12 @@
         return buf.at[(p["c"], p["z"], p["y"], p["x"], *half, pl.ds(*part), slice(None))]
 
     sends = [[links.sem() for _ in range(5)] for _ in orders]
-    gets = [[links.sem() for _ in range(9)] for _ in orders]
+    gets = [[links.sem() for _ in range(10)] for _ in orders]
     for o, (part, (a, b, c)) in each:
         sizes = ({a: three}, {a: every, b: three}, {a: every, b: every, c: two}, {a: every, b: every}, {a: every, b: every, c: every})
         links.sent += [(sem, region(part, **size)) for sem, size in zip(sends[o], sizes)]
-        handed.append((gets[o][8], region(part, **sizes[4])))
+        handed[0].append((gets[o][8], region(part, **{a: every, b: every, c: three})))
+        handed[1].append((gets[o][9], region(part, **{a: every, b: every})))
     rows = [[] for _ in orders]
 
     def send(o, kind, get, axis, step, **index):
@@ -94,10 +110,10 @@
         for k in (1, 3):
             send(o, 3, 7, c, k, **{**rows[o][j], a: halves[k], c: links.at(c, 4 - k)})
 
-    def hand(o, **index):
+    def hand(o, step):
         a, b, c = orders[o]
-        src = region(parts[o], **{a: every, b: every, **index})
-        links.copy(src, src, other, sends[o][4], gets[o][8])
+        src = region(parts[o], **{a: every, b: every, c: links.at(c, step)})
+        links.copy(src, src, other, sends[o][4], gets[o][9 if step == 2 else 8])
 
     for o, (part, (a, b, c)) in each:
         for k in (1, 3, 2):
@@ -119,18 +135,18 @@
     for o, (part, (a, b, c)) in each:
         wait(o, 2, **{a: every})
         spread(o, {a: every, b: links.at(b, 2)})
-        hand(o)
+        hand(o, 0)
     yield
     for j in (1, 2, 3):
         for o, _ in each:
             forward(o, j)
     for k in (1, 3):
         for o, (part, (a, b, c)) in each:
-            hand(o, **{c: links.at(c, 4 - k)})
+            hand(o, 4 - k)
     yield
     for o, (part, (a, b, c)) in each:
         wait(o, 7, **{a: every, b: every})
-        hand(o, **{c: links.at(c, 2)})
+        hand(o, 2)
 
 
 class Reduce:
@@ -245,6 +261,38 @@
         return jnp.concatenate(totals, axis=0)
 
 
+def over_blocks(links, colour, near, body, state):
+    columns = links.columns(colour)
+    pos = {n: jnp.where(colour == links.pos["c"], links.pos[n], links.twin[n]) for n in "xyz"}
+    pairs = [(dy, dx) for dy in range(4) for dx in range(4)]
+
+    def visit(state, dz, pairs):
+        for dy, dx in pairs:
+            where = [lax.rem(pos[n] + d, 4) for n, d in zip("zyx", (dz, dy, dx))]
+            state = body(state, where, columns(*where))
+        return state
+
+    if not near:
+        state = visit(state, 2, pairs)
+    pairs = [p for p in pairs if (2 not in p) == near]
+    return lax.fori_loop(0, 3, lambda i, state: visit(state, i + i // 2, pairs), state)
+
+
+def gather_and_sum(links, gathers, handed, body, state):
+    mine = links.pos["c"]
+    state = over_blocks(links, mine, True, body(mine), state)
+    for sem, like in handed[0]:
+        links.wait(sem, like)
+    state = over_blocks(links, 1 - mine, True, body(1 - mine), state)
+    for both in gathers:
+        for _ in both:
+            pass
+    state = over_blocks(links, mine, False, body(mine), state)
+    for sem, like in handed[1]:
+        links.wait(sem, like)
+    return over_blocks(links, 1 - mine, False, body(1 - mine), state)
+
+
 def factor_steps(work, first, last):
     lane = lax.broadcasted_iota(jnp.int32, (8, 128), 1)
     row = lax.broadcasted_iota(jnp.int32, (8, 1), 0)
@@ -271,7 +319,7 @@
     lax.fori_loop(first, last, panel_step, 0)
 
 
-def kernel(act, start, new_ref, sketch_ref, a_v, s_all, t_all, out_d, in_d, work, fac, proj_t,
+def kernel(act, start, new_ref, sketch_ref, a_v, s_all, t_all, out_d, in_d, work, held, fac, proj_t,
            h_all, h_in, h_mid, h_out, *rest):
     bufs = [[rest[18 * h + 6 * o : 18 * h + 6 * o + 6] for o in range(3)] for h in range(2)]
     local_sem, sems = rest[36:]
@@ -280,8 +328,11 @@
     c, z, y, x = pos["c"], pos["z"], pos["y"], pos["x"]
     chunk = 4096
 
-    load_s = pltpu.make_async_copy(start, s_all.at[c, z, y, x], local_sem.at[8])
-    load_s.start()
+    load_s = []
+    for h in range(2):
+        rows = pl.ds(h * 128, 128)
+        load_s.append(pltpu.make_async_copy(start.at[rows], s_all.at[c, z, y, x, h], local_sem.at[8 + h]))
+        load_s[h].start()
     loads = []
     for i in range(8):
         cols = pl.ds(i * chunk, chunk)
@@ -295,76 +346,96 @@
         pl.semaphore_signal(barrier, 1, device_id=device, device_id_type=MESH)
     pl.semaphore_wait(barrier, len(near))
 
-    load_s.wait()
-    handed = []
-    for _ in gather(links, s_all, START_PARTS, ORDERS, handed):
-        pass
+    for load in load_s:
+        load.wait()
+    handed = [[], []]
+    gathers = [gather(links, s_all, PARTS[h], ORDERS, handed, (h,)) for h in range(2)]
+    for _ in range(5):
+        next(gathers[0])
+        next(gathers[1])
     for load in loads:
         load.wait()
 
     def project(colour):
-        def body(i, total):
-            cols = pl.ds(pl.multiple_of((i * 2 + colour) * chunk, chunk), chunk)
-            return total + dot(a_v[:, cols], s_all[colour, i].reshape(chunk, 128))
+        def body(total, where, cols):
+            piece = s_all[(colour, *where)].reshape(256, 128)
+            return total + dot(a_v[:, cols], piece)
+
         return body
 
-    total = lax.fori_loop(0, 4, project(c), jnp.zeros((256, 128), F32))
-    for sem, like in handed:
-        links.wait(sem, like)
-    total = lax.fori_loop(0, 4, project(1 - c), total)
+    total = gather_and_sum(links, gathers, handed, project, jnp.zeros((256, 128), F32))
     proj_t[...] = total.T.astype(BF16)
 
-    def block(colour, zz, yx):
-        cols = pl.ds(pl.multiple_of((zz * 32 + colour * 16 + yx) * 256, 256), 256)
-        return dot(proj_t[...], a_v[:, cols])
-
-    pair = [links.sem() for _ in range(4)]
+    pair = [links.sem() for _ in range(8)]
     pair_sent = links.sem()
     links.sent.append((pair_sent, out_d))
-    order = [links.at("z", step) for step in (2, 1, 3, 0)]
-    given = []
-
-    def give():
-        zz = order[len(given)]
+    order = [links.at("z", step) for step in Reduce.steps]
+    order_other = [lax.rem(links.twin["z"] + step, 4) for step in Reduce.steps]
+
+    def plane(colour, zz, store):
+        columns = links.columns(colour)
         for i in range(16):
-            piece = block(1 - c, zz, i).astype(BF16)
+            piece = dot(proj_t[...], a_v[:, columns(zz, i // 4, i % 4)])
+            store(i // 4, i % 4, piece[:, :128], piece[:, 128:])
+
+    def give(n):
+        zz = order_other[n]
+
+        def store(u, v, *pieces):
             for h in range(2):
-                out_d[zz, i // 4, i % 4, h] = piece[:, h * 128 : h * 128 + 128]
-        links.copy(out_d.at[zz], in_d.at[zz], links.device(c=1 - c), pair_sent, pair[len(given)])
-        given.append(zz)
-
-    def produce(n):
-        while len(given) < min(n + 2, 4):
-            give()
+                out_d[h, zz, u, v] = pieces[h].astype(BF16)
+
+        plane(1 - c, zz, store)
+        for h in range(2):
+            src = out_d.at[h, zz]
+            given.append((src, in_d.at[h, zz], links.device(c=1 - c), pair_sent, pair[4 * h + n]))
+
+    def own(n):
         zz = order[n]
-        links.wait(pair[n], in_d.at[zz])
+        links.wait(pair[n], in_d.at[0, zz])
+        for m in ((), (), (0,), (1, 2, 3))[n]:
+            links.copy(*given[2 * m + 1])
+
+        def store(u, v, first, second):
+            work[zz, u, v, 0] = (first + in_d[0, zz, u, v].astype(F32)).astype(BF16)
+            held[zz, u, v] = second
+
+        plane(c, zz, store)
+
+    def own_second(n):
+        zz = order[n]
+        links.wait(pair[4 + n], in_d.at[1, zz])
         for i in range(16):
             u, v = i // 4, i % 4
-            piece = block(c, zz, i)
-            for h in range(2):
-                mine = piece[:, h * 128 : h * 128 + 128] + in_d[zz, u, v, h].astype(F32)
-                work[zz, u, v, h] = mine.astype(BF16)
-
-    handed, pulled_t, gathers = [], [None, None], [None, None]
-    sums = [Reduce(links, work, h, bufs[h], PANEL_PARTS[h], ORDERS) for h in range(2)]
+            work[zz, u, v, 1] = (held[zz, u, v] + in_d[1, zz, u, v].astype(F32)).astype(BF16)
+
+    handed, pulled_t, gathers = [[], []], [None, None], [None, None]
+    sums = [Reduce(links, work, h, bufs[h], PARTS[h], ORDERS) for h in range(2)]
 
     def done(h):
         pulled_t[h] = sums[h].finish()
         t_all[c, z, y, x, h] = pulled_t[h].astype(BF16)
-        gathers[h] = gather(links, t_all, PANEL_PARTS[h], ORDERS, handed, (h,))
+        gathers[h] = gather(links, t_all, PARTS[h], ORDERS, handed, (h,))
         next(gathers[h])
 
+    given = []
     for n in range(4):
-        produce(n)
+        give(n)
+        links.copy(*given[2 * n])
+    for n in range(4):
+        own(n)
         sums[0].start(n)
+    sums[0].forward()
+    for n in range(4):
+        own_second(n)
     sums[1].start()
-    sums[0].forward()
+    sums[0].own()
     sums[1].forward()
-    sums[0].own()
+    sums[0].last_axis()
     sums[1].own()
-    sums[0].last_axis()
+    done(0)
     sums[1].last_axis()
-    done(0)
+    next(gathers[0])
     done(1)
     next(gathers[0])
     next(gathers[1])
@@ -372,39 +443,29 @@
     next(gathers[1])
     next(gathers[0])
     next(gathers[1])
-    for _ in gathers[0]:
-        pass
-    for _ in gathers[1]:
-        pass
+    next(gathers[1])
     pulled_t = jnp.concatenate(pulled_t, axis=1)
 
     NT = (((1,), (1,)), ((), ()))
 
-    def gather_sums(colour):
-        def body(i, sums):
-            raw, gram = sums
-            for u in range(16):
-                piece = jnp.concatenate([t_all[colour, i, u // 4, u % 4, h] for h in range(2)], axis=1)
-                cols = pl.ds(pl.multiple_of((i * 32 + colour * 16 + u) * 256, 256), 256)
-                raw = raw + dot(a_v[:, cols], piece, NT)
-                gram = gram + dot(piece, piece, NT)
-            return raw, gram
+    def raw_and_squares(colour):
+        def body(sums, where, cols):
+            raw, squares = sums
+            halves = [t_all[(colour, *where, h)] for h in range(2)]
+            for half in halves:
+                squares = squares + half.astype(F32) * half.astype(F32)
+            return raw + dot(a_v[:, cols], jnp.concatenate(halves, axis=1), NT), squares
+
         return body
 
-    sums = (jnp.zeros((256, 128), F32), jnp.zeros((128, 128), F32))
-    sums = lax.fori_loop(0, 4, gather_sums(c), sums)
-    for sem, like in handed:
-        links.wait(sem, like)
-    raw, gram = lax.fori_loop(0, 4, gather_sums(1 - c), sums)
+    zeros = (jnp.zeros((256, 128), F32), jnp.zeros((128, 128), F32))
+    raw, squares = gather_and_sum(links, gathers, handed, raw_and_squares, zeros)
 
     rows = lax.broadcasted_iota(jnp.int32, (128, 128), 0)
     cols = lax.broadcasted_iota(jnp.int32, (128, 128), 1)
     eye = rows == cols
-    diagonal = jnp.where(eye, gram, 0.0)
-    d_row = 1.0 / jnp.sqrt(jnp.sum(diagonal, axis=0, keepdims=True))
-    d_col = 1.0 / jnp.sqrt(jnp.sum(diagonal, axis=1, keepdims=True))
-    fac[:, :128] = gram * d_row * d_col
-    fac[:, 128:] = jnp.where(eye, 1.0, 0.0).astype(F32)
+    d_col = 1.0 / jnp.sqrt(jnp.sum(squares, axis=1, keepdims=True))
+    d_row = jnp.sum(jnp.where(eye, d_col, 0.0), axis=0, keepdims=True)
     raw = raw * d_row
     h_all[...] = dot(raw, raw, (((0,), (0,)), ((), ())), HIGHEST)
 
@@ -416,17 +477,26 @@
         s = lax.rem(seq + k, 8)
         src = h_all.at[pl.ds(pl.multiple_of(s * 16, 16), 16)]
         links.copy(src, h_in.at[k - 1], (s, dp), sent[0], got[0])
-    factor_steps(fac, 0, 5)
+
+    def add_gram(i, gram):
+        for u in range(16):
+            piece = jnp.concatenate([t_all[i // 4, i % 4, u // 4, u % 4, h] for h in range(2)], axis=1)
+            gram = gram + dot(piece, piece, NT)
+        return gram
+
+    gram = lax.fori_loop(0, 8, add_gram, jnp.zeros((128, 128), F32))
+    fac[:, :128] = gram * d_row * d_col
+    fac[:, 128:] = jnp.where(eye, 1.0, 0.0).astype(F32)
     links.wait(got[0], h_in)
     h_mid[0] = h_all[here] + jnp.sum(h_in[...], axis=0)
     for k in range(1, 16):
         links.copy(h_mid.at[0], h_mid.at[k], (seq, lax.rem(dp + k, 16)), sent[1], got[1])
-    factor_steps(fac, 5, 11)
+    factor_steps(fac, 0, 8)
     links.wait(got[1], h_mid.at[pl.ds(1, 15)])
     h_out[here] = jnp.sum(h_mid[...], axis=0)
     for k in range(1, 8):
         links.copy(h_out.at[here], h_out.at[here], (lax.rem(seq + k, 8), dp), sent[2], got[2])
-    factor_steps(fac, 11, 16)
+    factor_steps(fac, 8, 16)
     inverse = fac[:, 128:]
     panel = dot(inverse, pulled_t * d_col, precision=HIGHEST).T.astype(BF16)
     new_ref[...] = panel
@@ -437,9 +507,17 @@
     shifted = ritz - jnp.where(eye, mean, 0.0)
     sign = shifted / (jnp.sqrt(jnp.sum(shifted * shifted)) + 1e-6)
 
+    def split(a):
+        high = a.astype(BF16)
+        return high, (a - high.astype(F32)).astype(BF16)
+
+    def product(a, b):
+        return dot(a[0], b[0]) + (dot(a[0], b[1]) + dot(a[1], b[0]))
+
     def sweep(_, sign):
-        square = dot(sign, sign, precision=HIGHEST)
-        return 0.5 * (3.0 * sign - dot(square, sign, precision=HIGHEST))
+        parts = split(sign)
+        square = product(parts, parts)
+        return 0.5 * (3.0 * sign - product(split(square), parts))
 
     sign = lax.fori_loop(0, NS_STEPS, sweep, sign)
     positive = 0.5 * (shifted + dot(shifted, sign, precision=HIGHEST))
@@ -450,11 +528,12 @@
 def local(activations, start_panel):
     scratch = [
         pltpu.VMEM((256, 32768), BF16),
-        pltpu.VMEM((2, 4, 4, 4, 256, 128), BF16),
         pltpu.VMEM((2, 4, 4, 4, 2, 128, 128), BF16),
+        pltpu.VMEM((2, 4, 4, 4, 2, 128, 128), BF16),
+        pltpu.VMEM((2, 4, 4, 4, 128, 128), BF16),
+        pltpu.VMEM((2, 4, 4, 4, 128, 128), BF16),
         pltpu.VMEM((4, 4, 4, 2, 128, 128), BF16),
-        pltpu.VMEM((4, 4, 4, 2, 128, 128), BF16),
-        pltpu.VMEM((4, 4, 4, 2, 128, 128), BF16),
+        pltpu.VMEM((4, 4, 4, 128, 128), F32),
         pltpu.VMEM((128, 256), F32),
         pltpu.VMEM((128, 256), BF16),
         pltpu.VMEM((128, 128), F32),
@@ -462,7 +541,7 @@
         pltpu.VMEM((16, 16, 128), F32),
         pltpu.VMEM((128, 128), F32),
     ]
-    for parts in PANEL_PARTS:
+    for parts in PARTS:
         for (_, rows), order in zip(parts, ORDERS):
             along_z = order[2] == "z"
             scratch += [
@@ -474,7 +553,7 @@
                 pltpu.VMEM((3, rows, 128), BF16),
             ]
     scratch += [
-        pltpu.SemaphoreType.DMA((9,)),
+        pltpu.SemaphoreType.DMA((10,)),
         pltpu.SemaphoreType.DMA((N_SEMS,)),
     ]
     return pl.pallas_call(

time: 123 us -> 117 us (0.951)
  Pallas kernels: 120 us -> 113 us
    pallas_call x1, Pallas kernels: 120 us -> 113 us  [local(): pl.pallas_call(kernel, out_shape=(jax.ShapeDtypeStruct((256, 128), BF16),...]
where the time goes in v3:
time: 117 us
  Pallas kernels  113 us (97%)
  local copies, waits for them, and re-layouts  3.04 us (3%)
    pallas_call x1, Pallas kernels, local(): pl.pallas_call(kernel, out_shape=(jax.ShapeDtypeStruct((256, 128), BF16),...  113 us
    unnamed x2, local copies, waits for them, and re-layouts  3.04 us

profile of v3, /device:TPU:1, one launch (start us, length us, event | category | flops | bytes accessed | tf_op | source)
XLA Modules:
  0.0 117.0 jit_solution(9537673561835070952)
XLA Ops:
  0.6 113.3 %subspace.1 = (bf16[256,128]{1,0:T(8,128)(2,1)}, f32[256,128]{1,0:T(8,128)}) custom-call(bf16[256,32768]{1,0:T(8,128)(2,1)} %act.1, bf16[256,128]{1,0:T(8,128)(2,1)} %start.1), custom_call_target="tpu_custom_call" | custom-call | tf_op jit(solution)/shard_map/subspace/pallas_call | solution.py:559
  114.0 1.5 %copy.6 = bf16[256,128]{1,0:T(8,128)(2,1)} copy(bf16[256,128]{1,0:T(8,128)(2,1)} %get-tuple-element.4) | data formatting | bytes 131072
  115.4 1.6 %copy.7 = f32[256,128]{1,0:T(8,128)} copy(f32[256,128]{1,0:T(8,128)} %get-tuple-element.5) | data formatting | bytes 262144

commit v4 on v3

--- a/solution.py
+++ b/solution.py
@@ -13,7 +13,7 @@
 HIGHEST = lax.Precision.HIGHEST
 ORDERS = (("x", "y", "z"), ("z", "x", "y"), ("y", "z", "x"))
 PARTS = (((0, 48), (48, 32), (80, 48)), ((0, 32), (32, 48), (80, 48)))
-N_SEMS = 4 * 45 + 2 * 24 + 9 + 6
+N_SEMS = 4 * 45 + 2 * 33 + 4 + 6
 
 
 def dot(a, b, dims=(((1,), (0,)), ((), ())), precision=None):
@@ -44,12 +44,13 @@
         z = jnp.where(first, p["z"], p["y"])
         return (z * 2 + p["c"], y * 4 + x)
 
-    def columns(self, colour):
+    def columns(self, colour, apart=False):
         first = colour == 0
-        strides = [jnp.where(first, a, b) for a, b in ((32, 1), (4, 32), (1, 4))]
+        wide, offset = (16, 0) if apart else (32, colour * 16)
+        strides = [jnp.where(first, a, b) for a, b in ((wide, 1), (4, wide), (1, 4))]
 
         def columns(*where):
-            place = colour * 16 + sum(i * stride for i, stride in zip(where, strides))
+            place = offset + sum(i * stride for i, stride in zip(where, strides))
             return pl.ds(pl.multiple_of(place * 256, 256), 256)
 
         return columns
@@ -160,6 +161,7 @@
         self.each = list(enumerate(zip(parts, orders)))
         self.sends = [[links.sem() for _ in range(4)] for _ in orders]
         self.gets = [[links.sem() for _ in range(4)] for _ in orders]
+        self.plane_gets = [[self.gets[o][0]] + [links.sem() for _ in range(3)] for o in range(3)]
         two, three = pl.ds(0, 2), pl.ds(0, 3)
         self.sizes = []
         for o, (part, (c, b, a)) in self.each:
@@ -183,39 +185,40 @@
     def wait(self, o, kind):
         self.links.wait(self.gets[o][kind], self.sizes[o][kind])
 
-    def start(self, n=None):
-        links = self.links
+    def start(self, n):
+        links, z = self.links, self.links.at("z", self.steps[n])
         for o, (part, (c, b, a)) in self.each:
             via = self.bufs[o][0]
             left = "x" if a == "y" else "y"
-            if a == "z" and n not in (None, 0):
+            if a == "z" and n:
                 continue
             for i, k in enumerate((1, 3)):
-                index, dst = {a: links.at(a, 2), left: self.halves[k]}, via.at[i]
-                if a != "z" and n is not None:
-                    z = links.at("z", self.steps[n])
-                    index["z"], dst = z, via.at[i, z]
-                self.send(o, 0, self.region(part, **index), dst, a, links.at(a, k))
-
-    def forward(self):
-        links, work = self.links, self.work
+                src = self.region(part, **{"z": z, a: links.at(a, 2), left: self.halves[k]})
+                dst = via.at[i] if a == "z" else via.at[i, z]
+                to = links.device(**{a: links.at(a, k)})
+                links.copy(src, dst, to, self.sends[o][0], self.plane_gets[o][n])
+
+    def forward(self, n):
+        links, work, z = self.links, self.work, self.links.at("z", self.steps[n])
         for o, (part, (c, b, a)) in self.each:
+            if a == "z" and n:
+                continue
             via, got = self.bufs[o][:2]
-            self.wait(o, 0)
+            like = {a: 0} if a == "z" else {a: 0, "z": 0}
+            links.wait(self.plane_gets[o][n], self.region(part, **like))
             for i, k in enumerate((1, 3)):
                 there = links.at(a, k)
-                for u in range(4):
-                    for j in range(2):
-                        v = 2 * i + j
-                        if a == "z":
-                            block, piece = dict(z=there, y=v, x=u), via[i, j, u]
-                        elif a == "y":
-                            block, piece = dict(z=u, y=there, x=v), via[i, u, j]
-                        else:
-                            block, piece = dict(z=u, y=v, x=there), via[i, u, j]
+                for j in range(2):
+                    v = 2 * i + j
+                    if a == "z":
+                        blocks = [(dict(z=there, y=v, x=u), (i, j, u)) for u in range(4)]
+                    else:
+                        blocks = [(dict(z=z, y=there, x=v) if a == "y" else dict(z=z, y=v, x=there), (i, z, j))]
+                    for block, piece in blocks:
                         where = self.at(part, **block)
-                        work[where] = (work[where].astype(F32) + piece.astype(F32)).astype(BF16)
-                self.send(o, 1, self.region(part, **{a: there}), got.at[i], a, there)
+                        work[where] = (work[where].astype(F32) + via[piece].astype(F32)).astype(BF16)
+                index, dst = ({a: there}, got.at[i]) if a == "z" else ({a: there, "z": z}, got.at[i, z])
+                self.send(o, 1, self.region(part, **index), dst, a, there)
 
     def own(self):
         links, pos = self.links, self.links.pos
@@ -319,7 +322,7 @@
     lax.fori_loop(first, last, panel_step, 0)
 
 
-def kernel(act, start, new_ref, sketch_ref, a_v, s_all, t_all, out_d, in_d, work, held, fac, proj_t,
+def kernel(act, start, new_ref, positive_ref, a_v, s_all, t_all, a_pair, proj_pair, work, fac, proj_t,
            h_all, h_in, h_mid, h_out, *rest):
     bufs = [[rest[18 * h + 6 * o : 18 * h + 6 * o + 6] for o in range(3)] for h in range(2)]
     local_sem, sems = rest[36:]
@@ -346,6 +349,12 @@
         pl.semaphore_signal(barrier, 1, device_id=device, device_id_type=MESH)
     pl.semaphore_wait(barrier, len(near))
 
+    twin = links.device(c=1 - c)
+    rows_sent, rows_got = links.sem(), links.sem()
+    links.sent.append((rows_sent, a_pair))
+    for i in range(4):
+        src = act.at[:, pl.ds(pl.multiple_of((2 * i + 1 - c) * chunk, chunk), chunk)]
+        links.copy(src, a_pair.at[:, pl.ds(i * chunk, chunk)], twin, rows_sent, rows_got)
     for load in load_s:
         load.wait()
     handed = [[], []]
@@ -366,48 +375,19 @@
     total = gather_and_sum(links, gathers, handed, project, jnp.zeros((256, 128), F32))
     proj_t[...] = total.T.astype(BF16)
 
-    pair = [links.sem() for _ in range(8)]
-    pair_sent = links.sem()
-    links.sent.append((pair_sent, out_d))
-    order = [links.at("z", step) for step in Reduce.steps]
-    order_other = [lax.rem(links.twin["z"] + step, 4) for step in Reduce.steps]
-
-    def plane(colour, zz, store):
-        columns = links.columns(colour)
+    proj_sent, proj_got = links.sem(), links.sem()
+    links.sent.append((proj_sent, proj_t))
+    links.copy(proj_t, proj_pair, twin, proj_sent, proj_got)
+    links.wait(rows_got, a_pair)
+    links.wait(proj_got, proj_pair)
+    columns, columns_pair = links.columns(c), links.columns(c, apart=True)
+
+    def plane(zz):
         for i in range(16):
-            piece = dot(proj_t[...], a_v[:, columns(zz, i // 4, i % 4)])
-            store(i // 4, i % 4, piece[:, :128], piece[:, 128:])
-
-    def give(n):
-        zz = order_other[n]
-
-        def store(u, v, *pieces):
+            where = (zz, i // 4, i % 4)
+            piece = dot(proj_t[...], a_v[:, columns(*where)]) + dot(proj_pair[...], a_pair[:, columns_pair(*where)])
             for h in range(2):
-                out_d[h, zz, u, v] = pieces[h].astype(BF16)
-
-        plane(1 - c, zz, store)
-        for h in range(2):
-            src = out_d.at[h, zz]
-            given.append((src, in_d.at[h, zz], links.device(c=1 - c), pair_sent, pair[4 * h + n]))
-
-    def own(n):
-        zz = order[n]
-        links.wait(pair[n], in_d.at[0, zz])
-        for m in ((), (), (0,), (1, 2, 3))[n]:
-            links.copy(*given[2 * m + 1])
-
-        def store(u, v, first, second):
-            work[zz, u, v, 0] = (first + in_d[0, zz, u, v].astype(F32)).astype(BF16)
-            held[zz, u, v] = second
-
-        plane(c, zz, store)
-
-    def own_second(n):
-        zz = order[n]
-        links.wait(pair[4 + n], in_d.at[1, zz])
-        for i in range(16):
-            u, v = i // 4, i % 4
-            work[zz, u, v, 1] = (held[zz, u, v] + in_d[1, zz, u, v].astype(F32)).astype(BF16)
+                work[(*where, h)] = piece[:, h * 128 : h * 128 + 128].astype(BF16)
 
     handed, pulled_t, gathers = [[], []], [None, None], [None, None]
     sums = [Reduce(links, work, h, bufs[h], PARTS[h], ORDERS) for h in range(2)]
@@ -418,19 +398,16 @@
         gathers[h] = gather(links, t_all, PARTS[h], ORDERS, handed, (h,))
         next(gathers[h])
 
-    given = []
+    for n, step in enumerate(Reduce.steps):
+        plane(links.at("z", step))
+        sums[0].start(n)
     for n in range(4):
-        give(n)
-        links.copy(*given[2 * n])
+        sums[1].start(n)
     for n in range(4):
-        own(n)
-        sums[0].start(n)
-    sums[0].forward()
+        sums[0].forward(n)
     for n in range(4):
-        own_second(n)
-    sums[1].start()
+        sums[1].forward(n)
     sums[0].own()
-    sums[1].forward()
     sums[0].last_axis()
     sums[1].own()
     done(0)
@@ -521,8 +498,13 @@
 
     sign = lax.fori_loop(0, NS_STEPS, sweep, sign)
     positive = 0.5 * (shifted + dot(shifted, sign, precision=HIGHEST))
-    sketch_ref[...] = math.sqrt(32768) / mean * dot(panel.astype(F32), positive, precision=HIGHEST)
+    positive_ref[...] = math.sqrt(32768) / mean * positive
     links.drain()
+
+
+def finish(panel, positive, new_ref, sketch_ref):
+    new_ref[...] = panel[...]
+    sketch_ref[...] = dot(panel[...].astype(F32), positive[...], precision=HIGHEST)
 
 
 def local(activations, start_panel):
@@ -530,10 +512,9 @@
         pltpu.VMEM((256, 32768), BF16),
         pltpu.VMEM((2, 4, 4, 4, 2, 128, 128), BF16),
         pltpu.VMEM((2, 4, 4, 4, 2, 128, 128), BF16),
-        pltpu.VMEM((2, 4, 4, 4, 128, 128), BF16),
-        pltpu.VMEM((2, 4, 4, 4, 128, 128), BF16),
+        pltpu.VMEM((256, 16384), BF16),
+        pltpu.VMEM((128, 256), BF16),
         pltpu.VMEM((4, 4, 4, 2, 128, 128), BF16),
-        pltpu.VMEM((4, 4, 4, 128, 128), F32),
         pltpu.VMEM((128, 256), F32),
         pltpu.VMEM((128, 256), BF16),
         pltpu.VMEM((128, 128), F32),
@@ -556,11 +537,11 @@
         pltpu.SemaphoreType.DMA((10,)),
         pltpu.SemaphoreType.DMA((N_SEMS,)),
     ]
-    return pl.pallas_call(
+    panel, positive = pl.pallas_call(
         kernel,
         out_shape=(
             jax.ShapeDtypeStruct((256, 128), BF16),
-            jax.ShapeDtypeStruct((256, 128), F32),
+            jax.ShapeDtypeStruct((128, 128), F32),
         ),
         in_specs=[pl.BlockSpec(memory_space=pl.ANY)] * 2,
         out_specs=(pl.BlockSpec(memory_space=pltpu.VMEM),) * 2,
@@ -570,6 +551,16 @@
         ),
         name="subspace",
     )(activations, start_panel)
+    return pl.pallas_call(
+        finish,
+        out_shape=(
+            jax.ShapeDtypeStruct((256, 128), BF16),
+            jax.ShapeDtypeStruct((256, 128), F32),
+        ),
+        in_specs=[pl.BlockSpec(memory_space=pltpu.VMEM)] * 2,
+        out_specs=(pl.BlockSpec(memory_space=pltpu.VMEM),) * 2,
+        name="finish",
+    )(panel, positive)
 
 
 def solution(mesh):

time: 117 us -> 112 us (0.957)
  local copies, waits for them, and re-layouts: 3.04 us -> 0 us
  Pallas kernels: 113 us -> 111 us
    pallas_call x1, Pallas kernels: 113 us -> 109 us  [local(): pl.pallas_call(kernel, out_shape=(jax.ShapeDtypeStruct((256, 128), BF16),...]
    unnamed x2 -> x0, local copies, waits for them, and re-layouts: 3.04 us -> none
    pallas_call x0 -> x1, Pallas kernels: none -> 1.79 us  [local(): pl.pallas_call(finish, out_shape=(jax.ShapeDtypeStruct((256, 128), BF16),...]
where the time goes in v4:
time: 112 us; the launch traced here: 111 us
  Pallas kernels  111 us (99%)
    pallas_call x1, Pallas kernels, local(): pl.pallas_call(kernel, out_shape=(jax.ShapeDtypeStruct((256, 128), BF16),...  109 us

profile of v4, /device:TPU:1, one launch (start us, length us, event | category | flops | bytes accessed | tf_op | source)
XLA Modules:
  0.0 111.4 jit_solution(5387361165820722345)
XLA Ops:
  0.6 108.9 %subspace.1 = (bf16[256,128]{1,0:T(8,128)(2,1)}, f32[128,128]{1,0:T(8,128)}) custom-call(bf16[256,32768]{1,0:T(8,128)(2,1)} %act.1, bf16[256,128]{1,0:T(8,128)(2,1)} %start.1), custom_call_target="tpu_custom_call" | custom-call | tf_op jit(solution)/shard_map/subspace/pallas_call | solution.py:540
  109.6 1.8 %finish.1 = (bf16[256,128]{1,0:T(8,128)(2,1)}, f32[256,128]{1,0:T(8,128)}) custom-call(bf16[256,128]{1,0:T(8,128)(2,1)} %get-tuple-element.4.panel, f32[128,128]{1,0:T(8,128)} %get-tuple-element.5.positive), custom_call_target="tpu_custom_call" | custom-call | tf_op jit(solution)/shard_map/finish/pallas_call | solution.py:554

commit v5 on v4

--- a/solution.py
+++ b/solution.py
@@ -13,7 +13,7 @@
 HIGHEST = lax.Precision.HIGHEST
 ORDERS = (("x", "y", "z"), ("z", "x", "y"), ("y", "z", "x"))
 PARTS = (((0, 48), (48, 32), (80, 48)), ((0, 32), (32, 48), (80, 48)))
-N_SEMS = 4 * 45 + 2 * 33 + 4 + 6
+N_SEMS = 4 * 48 + 2 * 33 + 4 + 6
 
 
 def dot(a, b, dims=(((1,), (0,)), ((), ())), precision=None):
@@ -84,7 +84,7 @@
         return buf.at[(p["c"], p["z"], p["y"], p["x"], *half, pl.ds(*part), slice(None))]
 
     sends = [[links.sem() for _ in range(5)] for _ in orders]
-    gets = [[links.sem() for _ in range(10)] for _ in orders]
+    gets = [[links.sem() for _ in range(11)] for _ in orders]
     for o, (part, (a, b, c)) in each:
         sizes = ({a: three}, {a: every, b: three}, {a: every, b: every, c: two}, {a: every, b: every}, {a: every, b: every, c: every})
         links.sent += [(sem, region(part, **size)) for sem, size in zip(sends[o], sizes)]
@@ -109,22 +109,22 @@
         a, b, c = orders[o]
         wait(o, 3 + j, **{a: every, c: two})
         for k in (1, 3):
-            send(o, 3, 7, c, k, **{**rows[o][j], a: halves[k], c: links.at(c, 4 - k)})
-
-    def hand(o, step):
+            send(o, 3, 10 if j == 3 else 7, c, k, **{**rows[o][j], a: halves[k], c: links.at(c, 4 - k)})
+
+    def hand(o, step, **row):
         a, b, c = orders[o]
-        src = region(parts[o], **{a: every, b: every, c: links.at(c, step)})
+        src = region(parts[o], **{a: every, b: every, c: links.at(c, step), **row})
         links.copy(src, src, other, sends[o][4], gets[o][9 if step == 2 else 8])
 
     for o, (part, (a, b, c)) in each:
-        for k in (1, 3, 2):
+        for k in (2, 1, 3):
             send(o, 0, 0, a, k)
     yield
     for o, (part, (a, b, c)) in each:
         wait(o, 0, **{a: three})
         for k in (1, 3, 2):
             send(o, 1, 2 if k == 2 else 1, b, k, **{a: every})
-        spread(o, {a: every})
+        spread(o, {a: every, b: pos[b]})
     yield
     for o, (part, (a, b, c)) in each:
         wait(o, 1, **{a: every, b: two})
@@ -146,8 +146,13 @@
             hand(o, 4 - k)
     yield
     for o, (part, (a, b, c)) in each:
-        wait(o, 7, **{a: every, b: every})
-        hand(o, 2)
+        wait(o, 7, **{a: every, b: three})
+        for row in rows[o][:3]:
+            hand(o, 2, **row)
+    yield
+    for o, (part, (a, b, c)) in each:
+        wait(o, 10, **{a: every})
+        hand(o, 2, **rows[o][3])
 
 
 class Reduce:
@@ -270,10 +275,11 @@
     pairs = [(dy, dx) for dy in range(4) for dx in range(4)]
 
     def visit(state, dz, pairs):
+        blocks = []
         for dy, dx in pairs:
             where = [lax.rem(pos[n] + d, 4) for n, d in zip("zyx", (dz, dy, dx))]
-            state = body(state, where, columns(*where))
-        return state
+            blocks.append((where, columns(*where)))
+        return body(state, blocks)
 
     if not near:
         state = visit(state, 2, pairs)
@@ -284,6 +290,8 @@
 def gather_and_sum(links, gathers, handed, body, state):
     mine = links.pos["c"]
     state = over_blocks(links, mine, True, body(mine), state)
+    for both in gathers:
+        next(both)
     for sem, like in handed[0]:
         links.wait(sem, like)
     state = over_blocks(links, 1 - mine, True, body(1 - mine), state)
@@ -366,9 +374,10 @@
         load.wait()
 
     def project(colour):
-        def body(total, where, cols):
-            piece = s_all[(colour, *where)].reshape(256, 128)
-            return total + dot(a_v[:, cols], piece)
+        def body(total, blocks):
+            pieces = [s_all[(colour, *where)].reshape(256, 128) for where, _ in blocks]
+            wide = jnp.concatenate([a_v[:, cols] for _, cols in blocks], axis=1)
+            return total + dot(wide, jnp.concatenate(pieces, axis=0))
 
         return body
 
@@ -382,10 +391,13 @@
     links.wait(proj_got, proj_pair)
     columns, columns_pair = links.columns(c), links.columns(c, apart=True)
 
+    proj_both = jnp.concatenate([proj_t[...], proj_pair[...]], axis=1)
+
     def plane(zz):
         for i in range(16):
             where = (zz, i // 4, i % 4)
-            piece = dot(proj_t[...], a_v[:, columns(*where)]) + dot(proj_pair[...], a_pair[:, columns_pair(*where)])
+            both = jnp.concatenate([a_v[:, columns(*where)], a_pair[:, columns_pair(*where)]], axis=0)
+            piece = dot(proj_both, both)
             for h in range(2):
                 work[(*where, h)] = piece[:, h * 128 : h * 128 + 128].astype(BF16)
 
@@ -426,12 +438,13 @@
     NT = (((1,), (1,)), ((), ()))
 
     def raw_and_squares(colour):
-        def body(sums, where, cols):
+        def body(sums, blocks):
             raw, squares = sums
-            halves = [t_all[(colour, *where, h)] for h in range(2)]
+            halves = [t_all[(colour, *where, h)] for where, _ in blocks for h in range(2)]
             for half in halves:
                 squares = squares + half.astype(F32) * half.astype(F32)
-            return raw + dot(a_v[:, cols], jnp.concatenate(halves, axis=1), NT), squares
+            wide = jnp.concatenate([a_v[:, cols] for _, cols in blocks], axis=1)
+            return raw + dot(wide, jnp.concatenate(halves, axis=1), NT), squares
 
         return body
 
@@ -450,28 +463,27 @@
     here = pl.ds(pl.multiple_of(seq * 16, 16), 16)
     sent, got = [links.sem() for _ in range(3)], [links.sem() for _ in range(3)]
     links.sent += [(sent[0], h_in), (sent[1], h_mid.at[pl.ds(1, 15)]), (sent[2], h_in)]
-    for k in range(1, 8):
+    for k in (4, 5, 3, 2, 6, 1, 7):
         s = lax.rem(seq + k, 8)
         src = h_all.at[pl.ds(pl.multiple_of(s * 16, 16), 16)]
         links.copy(src, h_in.at[k - 1], (s, dp), sent[0], got[0])
 
     def add_gram(i, gram):
-        for u in range(16):
-            piece = jnp.concatenate([t_all[i // 4, i % 4, u // 4, u % 4, h] for h in range(2)], axis=1)
-            gram = gram + dot(piece, piece, NT)
-        return gram
+        pieces = [t_all[i // 4, i % 4, u // 4, u % 4, h] for u in range(16) for h in range(2)]
+        wide = jnp.concatenate(pieces, axis=1)
+        return gram + dot(wide, wide, NT)
 
     gram = lax.fori_loop(0, 8, add_gram, jnp.zeros((128, 128), F32))
     fac[:, :128] = gram * d_row * d_col
     fac[:, 128:] = jnp.where(eye, 1.0, 0.0).astype(F32)
     links.wait(got[0], h_in)
     h_mid[0] = h_all[here] + jnp.sum(h_in[...], axis=0)
-    for k in range(1, 16):
+    for k in (10, 6, 9, 11, 14, 5, 7, 2, 8, 13, 15, 3, 4, 12, 1):
         links.copy(h_mid.at[0], h_mid.at[k], (seq, lax.rem(dp + k, 16)), sent[1], got[1])
     factor_steps(fac, 0, 8)
     links.wait(got[1], h_mid.at[pl.ds(1, 15)])
     h_out[here] = jnp.sum(h_mid[...], axis=0)
-    for k in range(1, 8):
+    for k in (4, 5, 3, 2, 6, 1, 7):
         links.copy(h_out.at[here], h_out.at[here], (lax.rem(seq + k, 8), dp), sent[2], got[2])
     factor_steps(fac, 8, 16)
     inverse = fac[:, 128:]

time: 112 us -> 112 us (level)
  no operation moved by 1% of the time
where the time goes in v5:
time: 112 us
  Pallas kernels  111 us (99%)
    pallas_call x1, Pallas kernels, local(): pl.pallas_call(kernel, out_shape=(jax.ShapeDtypeStruct((256, 128), BF16),...  109 us

profile of v5, /device:TPU:1, one launch (start us, length us, event | category | flops | bytes accessed | tf_op | source)
XLA Modules:
  0.0 111.6 jit_solution(4070385583758710790)
XLA Ops:
  0.6 109.2 %subspace.1 = (bf16[256,128]{1,0:T(8,128)(2,1)}, f32[128,128]{1,0:T(8,128)}) custom-call(bf16[256,32768]{1,0:T(8,128)(2,1)} %act.1, bf16[256,128]{1,0:T(8,128)(2,1)} %start.1), custom_call_target="tpu_custom_call" | custom-call | tf_op jit(solution)/shard_map/subspace/pallas_call | solution.py:552
  109.8 1.8 %finish.1 = (bf16[256,128]{1,0:T(8,128)(2,1)}, f32[256,128]{1,0:T(8,128)}) custom-call(bf16[256,128]{1,0:T(8,128)(2,1)} %get-tuple-element.4.panel, f32[128,128]{1,0:T(8,128)} %get-tuple-element.5.positive), custom_call_target="tpu_custom_call" | custom-call | tf_op jit(solution)/shard_map/finish/pallas_call | solution.py:566

commit v6 on v5

--- a/solution.py
+++ b/solution.py
@@ -13,7 +13,7 @@
 HIGHEST = lax.Precision.HIGHEST
 ORDERS = (("x", "y", "z"), ("z", "x", "y"), ("y", "z", "x"))
 PARTS = (((0, 48), (48, 32), (80, 48)), ((0, 32), (32, 48), (80, 48)))
-N_SEMS = 4 * 48 + 2 * 33 + 4 + 6
+N_SEMS = 4 * 26 + 2 * 22 + 4 + 6
 
 
 def dot(a, b, dims=(((1,), (0,)), ((), ())), precision=None):
@@ -21,14 +21,14 @@
 
 
 class Links:
-    def __init__(self, sems):
+    def __init__(self, sems, ruler):
         seq, dp = lax.axis_index("seq"), lax.axis_index("dp")
         x, y, z, c = dp % 4, dp // 4, seq // 2, seq % 2
         first = c == 0
         self.pos = dict(c=c, x=jnp.where(first, x, y), y=jnp.where(first, y, z), z=jnp.where(first, z, x))
         self.twin = dict(c=1 - c, x=jnp.where(first, y, x), y=jnp.where(first, z, y), z=jnp.where(first, x, z))
         self.seq, self.dp = seq, dp
-        self.sems, self.used, self.sent = sems, 0, []
+        self.sems, self.ruler, self.used, self.sent = sems, ruler, 0, []
 
     def sem(self):
         self.used += 1
@@ -68,6 +68,9 @@
     def wait(self, sem, like):
         pltpu.make_async_copy(like, like, self.sems.at[sem]).wait()
 
+    def blocks(self, count):
+        return self.ruler.at[pl.ds(0, 128), pl.ds(0, count * 128)]
+
     def drain(self):
         for sem, like in self.sent:
             self.wait(sem, like)
@@ -83,18 +86,16 @@
         p = {**pos, **index}
         return buf.at[(p["c"], p["z"], p["y"], p["x"], *half, pl.ds(*part), slice(None))]
 
-    sends = [[links.sem() for _ in range(5)] for _ in orders]
-    gets = [[links.sem() for _ in range(11)] for _ in orders]
-    for o, (part, (a, b, c)) in each:
-        sizes = ({a: three}, {a: every, b: three}, {a: every, b: every, c: two}, {a: every, b: every}, {a: every, b: every, c: every})
-        links.sent += [(sem, region(part, **size)) for sem, size in zip(sends[o], sizes)]
-        handed[0].append((gets[o][8], region(part, **{a: every, b: every, c: three})))
-        handed[1].append((gets[o][9], region(part, **{a: every, b: every})))
+    sends, first, early, late, last = [links.sem() for _ in range(5)]
+    gets = [[first] + [links.sem() for _ in range(6)] + [last, early, late, links.sem()] for _ in orders]
+    links.sent.append((sends, links.blocks(127)))
+    handed[0].append((early, links.blocks(48)))
+    handed[1].append((late, links.blocks(16)))
     rows = [[] for _ in orders]
 
-    def send(o, kind, get, axis, step, **index):
+    def send(o, get, axis, step, **index):
         src = region(parts[o], **index)
-        links.copy(src, src, links.device(**{axis: links.at(axis, step)}), sends[o][kind], gets[o][get])
+        links.copy(src, src, links.device(**{axis: links.at(axis, step)}), sends, gets[o][get])
 
     def wait(o, get, **size):
         links.wait(gets[o][get], region(parts[o], **size))
@@ -103,27 +104,27 @@
         a, b, c = orders[o]
         rows[o].append(row)
         for k in (1, 3):
-            send(o, 2, 2 + len(rows[o]), c, k, **row)
+            send(o, 2 + len(rows[o]), c, k, **row)
 
     def forward(o, j):
         a, b, c = orders[o]
         wait(o, 3 + j, **{a: every, c: two})
         for k in (1, 3):
-            send(o, 3, 10 if j == 3 else 7, c, k, **{**rows[o][j], a: halves[k], c: links.at(c, 4 - k)})
+            send(o, 10 if j == 3 else 7, c, k, **{**rows[o][j], a: halves[k], c: links.at(c, 4 - k)})
 
     def hand(o, step, **row):
         a, b, c = orders[o]
         src = region(parts[o], **{a: every, b: every, c: links.at(c, step), **row})
-        links.copy(src, src, other, sends[o][4], gets[o][9 if step == 2 else 8])
+        links.copy(src, src, other, sends, gets[o][9 if step == 2 else 8])
 
     for o, (part, (a, b, c)) in each:
         for k in (2, 1, 3):
-            send(o, 0, 0, a, k)
+            send(o, 0, a, k)
     yield
+    links.wait(first, links.blocks(3))
     for o, (part, (a, b, c)) in each:
-        wait(o, 0, **{a: three})
         for k in (1, 3, 2):
-            send(o, 1, 2 if k == 2 else 1, b, k, **{a: every})
+            send(o, 2 if k == 2 else 1, b, k, **{a: every})
         spread(o, {a: every, b: pos[b]})
     yield
     for o, (part, (a, b, c)) in each:
@@ -145,8 +146,8 @@
         for o, (part, (a, b, c)) in each:
             hand(o, 4 - k)
     yield
+    links.wait(last, links.blocks(12))
     for o, (part, (a, b, c)) in each:
-        wait(o, 7, **{a: every, b: three})
         for row in rows[o][:3]:
             hand(o, 2, **row)
     yield
@@ -164,7 +165,8 @@
         self.links, self.work, self.h, self.bufs = links, work, h, bufs
         self.parts, self.orders = parts, orders
         self.each = list(enumerate(zip(parts, orders)))
-        self.sends = [[links.sem() for _ in range(4)] for _ in orders]
+        self.sends = links.sem()
+        links.sent.append((self.sends, links.blocks(63)))
         self.gets = [[links.sem() for _ in range(4)] for _ in orders]
         self.plane_gets = [[self.gets[o][0]] + [links.sem() for _ in range(3)] for o in range(3)]
         two, three = pl.ds(0, 2), pl.ds(0, 3)
@@ -172,7 +174,6 @@
         for o, (part, (c, b, a)) in self.each:
             sum1, sum2 = bufs[o][2], bufs[o][4]
             likes = (self.region(part, **{a: 0}), self.region(part, **{a: two}), sum1.at[three], sum2.at[three])
-            links.sent += list(zip(self.sends[o], likes))
             self.sizes.append(likes)
 
     def at(self, part, **index):
@@ -185,7 +186,7 @@
 
     def send(self, o, kind, src, dst, axis, to):
         links = self.links
-        links.copy(src, dst, links.device(**{axis: to}), self.sends[o][kind], self.gets[o][kind])
+        links.copy(src, dst, links.device(**{axis: to}), self.sends, self.gets[o][kind])
 
     def wait(self, o, kind):
         self.links.wait(self.gets[o][kind], self.sizes[o][kind])
@@ -201,7 +202,7 @@
                 src = self.region(part, **{"z": z, a: links.at(a, 2), left: self.halves[k]})
                 dst = via.at[i] if a == "z" else via.at[i, z]
                 to = links.device(**{a: links.at(a, k)})
-                links.copy(src, dst, to, self.sends[o][0], self.plane_gets[o][n])
+                links.copy(src, dst, to, self.sends, self.plane_gets[o][n])
 
     def forward(self, n):
         links, work, z = self.links, self.work, self.links.at("z", self.steps[n])
@@ -334,7 +335,7 @@
            h_all, h_in, h_mid, h_out, *rest):
     bufs = [[rest[18 * h + 6 * o : 18 * h + 6 * o + 6] for o in range(3)] for h in range(2)]
     local_sem, sems = rest[36:]
-    links = Links(sems)
+    links = Links(sems, a_v)
     pos = links.pos
     c, z, y, x = pos["c"], pos["z"], pos["y"], pos["x"]
     chunk = 4096
@@ -480,12 +481,12 @@
     h_mid[0] = h_all[here] + jnp.sum(h_in[...], axis=0)
     for k in (10, 6, 9, 11, 14, 5, 7, 2, 8, 13, 15, 3, 4, 12, 1):
         links.copy(h_mid.at[0], h_mid.at[k], (seq, lax.rem(dp + k, 16)), sent[1], got[1])
-    factor_steps(fac, 0, 8)
+    factor_steps(fac, 0, 10)
     links.wait(got[1], h_mid.at[pl.ds(1, 15)])
     h_out[here] = jnp.sum(h_mid[...], axis=0)
     for k in (4, 5, 3, 2, 6, 1, 7):
         links.copy(h_out.at[here], h_out.at[here], (lax.rem(seq + k, 8), dp), sent[2], got[2])
-    factor_steps(fac, 8, 16)
+    factor_steps(fac, 10, 16)
     inverse = fac[:, 128:]
     panel = dot(inverse, pulled_t * d_col, precision=HIGHEST).T.astype(BF16)
     new_ref[...] = panel

time: 112 us -> 109 us (0.973)
  Pallas kernels: 111 us -> 108 us
    pallas_call x1, Pallas kernels: 109 us -> 106 us  [local(): pl.pallas_call(kernel, out_shape=(jax.ShapeDtypeStruct((256, 128), BF16),...]
where the time goes in v6:
time: 109 us
  Pallas kernels  108 us (99%)
    pallas_call x1, Pallas kernels, local(): pl.pallas_call(kernel, out_shape=(jax.ShapeDtypeStruct((256, 128), BF16),...  106 us

profile of v6, /device:TPU:1, one launch (start us, length us, event | category | flops | bytes accessed | tf_op | source)
XLA Modules:
  0.0 108.9 jit_solution(308365547602752888)
XLA Ops:
  0.6 106.4 %subspace.1 = (bf16[256,128]{1,0:T(8,128)(2,1)}, f32[128,128]{1,0:T(8,128)}) custom-call(bf16[256,32768]{1,0:T(8,128)(2,1)} %act.1, bf16[256,128]{1,0:T(8,128)(2,1)} %start.1), custom_call_target="tpu_custom_call" | custom-call | tf_op jit(solution)/shard_map/subspace/pallas_call | solution.py:553
  107.1 1.8 %finish.1 = (bf16[256,128]{1,0:T(8,128)(2,1)}, f32[256,128]{1,0:T(8,128)}) custom-call(bf16[256,128]{1,0:T(8,128)(2,1)} %get-tuple-element.4.panel, f32[128,128]{1,0:T(8,128)} %get-tuple-element.5.positive), custom_call_target="tpu_custom_call" | custom-call | tf_op jit(solution)/shard_map/finish/pallas_call | solution.py:567

commit v7 on v6

--- a/solution.py
+++ b/solution.py
@@ -13,7 +13,7 @@
 HIGHEST = lax.Precision.HIGHEST
 ORDERS = (("x", "y", "z"), ("z", "x", "y"), ("y", "z", "x"))
 PARTS = (((0, 48), (48, 32), (80, 48)), ((0, 32), (32, 48), (80, 48)))
-N_SEMS = 4 * 26 + 2 * 22 + 4 + 6
+N_SEMS = 4 * 12 + 2 * 22 + 4 + 6
 
 
 def dot(a, b, dims=(((1,), (0,)), ((), ())), precision=None):
@@ -87,7 +87,9 @@
         return buf.at[(p["c"], p["z"], p["y"], p["x"], *half, pl.ds(*part), slice(None))]
 
     sends, first, early, late, last = [links.sem() for _ in range(5)]
-    gets = [[first] + [links.sem() for _ in range(6)] + [last, early, late, links.sem()] for _ in orders]
+    near, far, *third = [links.sem() for _ in range(6)]
+    final = links.sem()
+    gets = [[first, near, far, *third, last, early, late, final] for _ in orders]
     links.sent.append((sends, links.blocks(127)))
     handed[0].append((early, links.blocks(48)))
     handed[1].append((late, links.blocks(16)))
@@ -96,9 +98,6 @@
     def send(o, get, axis, step, **index):
         src = region(parts[o], **index)
         links.copy(src, src, links.device(**{axis: links.at(axis, step)}), sends, gets[o][get])
-
-    def wait(o, get, **size):
-        links.wait(gets[o][get], region(parts[o], **size))
 
     def spread(o, row):
         a, b, c = orders[o]
@@ -108,7 +107,6 @@
 
     def forward(o, j):
         a, b, c = orders[o]
-        wait(o, 3 + j, **{a: every, c: two})
         for k in (1, 3):
             send(o, 10 if j == 3 else 7, c, k, **{**rows[o][j], a: halves[k], c: links.at(c, 4 - k)})
 
@@ -125,21 +123,24 @@
     for o, (part, (a, b, c)) in each:
         for k in (1, 3, 2):
             send(o, 2 if k == 2 else 1, b, k, **{a: every})
+    for o, (part, (a, b, c)) in each:
         spread(o, {a: every, b: pos[b]})
     yield
-    for o, (part, (a, b, c)) in each:
-        wait(o, 1, **{a: every, b: two})
+    links.wait(near, links.blocks(8))
+    for o, (part, (a, b, c)) in each:
         for step in (1, 3):
             spread(o, {a: every, b: links.at(b, 4 - step)})
     yield
+    links.wait(third[0], links.blocks(8))
     for o, _ in each:
         forward(o, 0)
-    for o, (part, (a, b, c)) in each:
-        wait(o, 2, **{a: every})
+    links.wait(far, links.blocks(4))
+    for o, (part, (a, b, c)) in each:
         spread(o, {a: every, b: links.at(b, 2)})
         hand(o, 0)
     yield
     for j in (1, 2, 3):
+        links.wait(third[j], links.blocks(8))
         for o, _ in each:
             forward(o, j)
     for k in (1, 3):
@@ -151,8 +152,8 @@
         for row in rows[o][:3]:
             hand(o, 2, **row)
     yield
-    for o, (part, (a, b, c)) in each:
-        wait(o, 10, **{a: every})
+    links.wait(final, links.blocks(4))
+    for o, (part, (a, b, c)) in each:
         hand(o, 2, **rows[o][3])
 
 
@@ -358,17 +359,19 @@
         pl.semaphore_signal(barrier, 1, device_id=device, device_id_type=MESH)
     pl.semaphore_wait(barrier, len(near))
 
+    for load in load_s:
+        load.wait()
+    handed = [[], []]
+    gathers = [gather(links, s_all, PARTS[h], ORDERS, handed, (h,)) for h in range(2)]
+    next(gathers[0])
+    next(gathers[1])
     twin = links.device(c=1 - c)
     rows_sent, rows_got = links.sem(), links.sem()
     links.sent.append((rows_sent, a_pair))
     for i in range(4):
         src = act.at[:, pl.ds(pl.multiple_of((2 * i + 1 - c) * chunk, chunk), chunk)]
         links.copy(src, a_pair.at[:, pl.ds(i * chunk, chunk)], twin, rows_sent, rows_got)
-    for load in load_s:
-        load.wait()
-    handed = [[], []]
-    gathers = [gather(links, s_all, PARTS[h], ORDERS, handed, (h,)) for h in range(2)]
-    for _ in range(5):
+    for _ in range(4):
         next(gathers[0])
         next(gathers[1])
     for load in loads:

time: 109 us -> 108 us (level)
  no operation moved by 1% of the time
where the time goes in v7:
time: 108 us
  Pallas kernels  108 us (100%)
    pallas_call x1, Pallas kernels, local(): pl.pallas_call(kernel, out_shape=(jax.ShapeDtypeStruct((256, 128), BF16),...  106 us

profile of v7, /device:TPU:1, one launch (start us, length us, event | category | flops | bytes accessed | tf_op | source)
XLA Modules:
  0.0 108.3 jit_solution(5898168113253996083)
XLA Ops:
  0.6 105.8 %subspace.1 = (bf16[256,128]{1,0:T(8,128)(2,1)}, f32[128,128]{1,0:T(8,128)}) custom-call(bf16[256,32768]{1,0:T(8,128)(2,1)} %act.1, bf16[256,128]{1,0:T(8,128)(2,1)} %start.1), custom_call_target="tpu_custom_call" | custom-call | tf_op jit(solution)/shard_map/subspace/pallas_call | solution.py:556
  106.5 1.8 %finish.1 = (bf16[256,128]{1,0:T(8,128)(2,1)}, f32[256,128]{1,0:T(8,128)}) custom-call(bf16[256,128]{1,0:T(8,128)(2,1)} %get-tuple-element.4.panel, f32[128,128]{1,0:T(8,128)} %get-tuple-element.5.positive), custom_call_target="tpu_custom_call" | custom-call | tf_op jit(solution)/shard_map/finish/pallas_call | solution.py:570
